TPU v7x, 128 devices: a whole 4x4x4 slice. The times are simulated.
128 devices in a mesh: frame: 16 (over x_lo, z, core), head: 8 (over y, x_hi).
Axes of the slice: x: 4 (x_hi: 2, x_lo: 2; x = x_hi * 2 + x_lo), y: 4, z: 4, core: 2. Of those that a mesh axis runs over, the one named last changes fastest.
Arguments:
- queries: bfloat16 [1024, 8192], P('frame', 'head'), may hold values from -6 to 6
- q_gain: float32 [128], replicated, may hold values from 0.1 to 1.9
- keys: bfloat16 [25600, 1024], P('frame', 'head'), may hold values from -6 to 6
- k_gain: float32 [128], replicated, may hold values from 0.1 to 1.9
- values: bfloat16 [25600, 1024], P('frame', 'head'), may hold values from -6 to 6
- out_grad: bfloat16 [1024, 8192], P('frame', 'head'), may hold values from -384 to 384
- w_query: bfloat16 [8192, 8192], P(None, 'head'), may hold values from -0.0625 to 0.0625
- span_mask: int32 [64, 16], P(None, 'frame'), may hold values from 0 to 1, as said below
- frame_len: int32 [16], P('frame'), may hold values from 400 to 1600
Outputs:
- text_grad: float32 [1024, 8192], P('frame', 'head')
- key_grad: float32 [25600, 1024], P('frame', 'head')
- value_grad: float32 [25600, 1024], P('frame', 'head')
Inputs may be any that keep to these rules, and one draw needn't show every extreme that they name: `span_mask`: every text span sees at least one frame.
All inputs are finite; a program needn't handle non-finite values.
Results may differ from a plain program's by a relative error of at most 0.012.
The roundings to bfloat16 on the way count: a program that leaves them out, or rounds other values in their place, can miss the bound.
Values may be sent and summed in bfloat16 or wider, within the bound.
A program may use at most 128 MiB of HBM per device.

v0:
```python
import jax
import jax.numpy as jnp
from jax import lax
from jax.sharding import PartitionSpec as P

BLK = 16


EPS = 1e-05


def sent_together(arrays, axis, dim, along):
    ends, at = ([], 0)
    for a in arrays[:-1]:
        at += a.shape[along]
        ends.append(at)
    both = jnp.concatenate(arrays, axis=along)
    return tuple(jnp.split(lax.all_gather(both, axis, axis=dim, tiled=True), ends, axis=along))


def copy_for_each(value, axis):
    copies = jnp.broadcast_to(value, (lax.axis_size(axis), *value.shape))
    return lax.all_to_all(copies, axis, split_axis=0, concat_axis=0, tiled=True)


def taken_together(value, axis):
    return copy_for_each(value, axis).sum(axis=0)


def in_one(arrays, axis):
    ends = [0]
    for a in arrays:
        ends.append(ends[-1] + a.size)
    subtotal = taken_together(jnp.concatenate([a.ravel() for a in arrays]), axis)
    return tuple((subtotal[b:e].reshape(a.shape) for a, b, e in zip(arrays, ends, ends[1:])))


def cut_along(value, dim, devices):
    before, after = (value.shape[:dim], value.shape[dim + 1 :])
    return jnp.moveaxis(value.reshape(*before, devices, -1, *after), dim, 0)


def summed_on_arrival(value, axis, dim):
    parts = cut_along(value, dim, lax.axis_size(axis))
    arrived = lax.all_to_all(parts, axis, split_axis=0, concat_axis=0, tiled=True)
    return arrived.astype(jnp.float32).sum(axis=0)


def norm_fwd(field, gain):
    scale = lax.rsqrt(jnp.mean(field * field, axis=-1, keepdims=True) + EPS)
    return (field * scale * gain, scale)


def norm_bwd(field, scale, grad):
    return scale * grad - field * scale**3 * jnp.mean(field * grad, axis=-1, keepdims=True)


def visible(span_col, rows, key_ok):
    spans = jnp.arange(rows, dtype=jnp.int32) // BLK
    hit = (spans[:, None] == jnp.arange(span_col.shape[0], dtype=jnp.int32)[None, :]) & (
        span_col[None, :] > 0
    )
    row_ok = jnp.any(hit, axis=1)
    return (row_ok[:, None] & key_ok[None, :], row_ok)


def block_scores(q_rows, d_rows, key_b, val_b, kv_heads, allowed):
    rows = q_rows.shape[0]
    head_size = key_b.shape[1] // kv_heads
    q_heads = q_rows.reshape(rows, kv_heads, -1, head_size)
    d_heads = d_rows.reshape(rows, kv_heads, -1, head_size)
    k_heads = key_b.reshape(-1, kv_heads, head_size)
    v_heads = val_b.reshape(-1, kv_heads, head_size)
    scores = jnp.einsum("rkgd,nkd->kgrn", q_heads, k_heads, preferred_element_type=jnp.float32)
    dprob = jnp.einsum("rkgd,nkd->kgrn", d_heads, v_heads, preferred_element_type=jnp.float32)
    expd = jnp.where(allowed[None, None], jnp.exp(scores), jnp.float32(0.0))
    return (expd, dprob, q_heads, d_heads, k_heads)


def block_stats(q_rows, d_rows, key_b, val_b, kv_heads, allowed):
    rows = q_rows.shape[0]
    expd, dprob, _, _, _ = block_scores(q_rows, d_rows, key_b, val_b, kv_heads, allowed)
    total = jnp.sum(expd, axis=-1).reshape(-1, rows)
    weighted = jnp.sum(expd * dprob, axis=-1).reshape(-1, rows)
    return (total, weighted)


def block_grads(q_rows, d_rows, key_b, val_b, kv_heads, allowed, total, weighted):
    rows = q_rows.shape[0]
    expd, dprob, q_heads, d_heads, k_heads = block_scores(
        q_rows, d_rows, key_b, val_b, kv_heads, allowed
    )
    tot = total.reshape(kv_heads, -1, rows)[..., None]
    mean_dp = weighted.reshape(kv_heads, -1, rows)[..., None] / tot
    prob = expd / tot
    dscore = prob * (dprob - mean_dp)
    prob_b = prob.astype(jnp.bfloat16)
    dscore_b = dscore.astype(jnp.bfloat16)
    dv_part = jnp.einsum("kgrn,rkgd->nkd", prob_b, d_heads, preferred_element_type=jnp.float32)
    dk_part = jnp.einsum("kgrn,rkgd->nkd", dscore_b, q_heads, preferred_element_type=jnp.float32)
    dq_part = jnp.einsum("kgrn,nkd->rkgd", dscore_b, k_heads, preferred_element_type=jnp.float32)
    return (dq_part.reshape(rows, -1), dk_part, dv_part)


def local(queries, q_gain, keys, k_gain, values, out_grad, w_query, span_mask, frame_len):
    rows, width = queries.shape
    head_size = q_gain.shape[0]
    q_heads = width // head_size
    kv_heads = keys.shape[1] // head_size
    key_rows = keys.shape[0]
    q_raw = queries.astype(jnp.float32).reshape(rows, q_heads, head_size)
    q_normed, q_scale = norm_fwd(q_raw, q_gain)
    q_b = (q_normed * head_size ** (-0.5)).astype(jnp.bfloat16).reshape(rows, width)
    k_raw = keys.astype(jnp.float32).reshape(key_rows, kv_heads, head_size)
    k_normed, k_scale = norm_fwd(k_raw, k_gain)
    k_b = k_normed.astype(jnp.bfloat16).reshape(key_rows, kv_heads * head_size)
    key_ok = jnp.arange(key_rows, dtype=jnp.int32) < frame_len[0]
    span_col = span_mask[:, 0]
    count = lax.axis_size("frame")
    zero_kv = jnp.zeros((key_rows, kv_heads, head_size), jnp.float32)
    q_all, d_all = sent_together((q_b, out_grad), "frame", 0, 1)
    every = rows * count
    per_block = max(1, min(count, 256 // rows))
    while count % per_block != 0:
        per_block -= 1
    block_rows = per_block * rows
    blocks = count // per_block
    _, row_ok_all = visible(span_col, every, key_ok)
    q_blocks = q_all.reshape(blocks, block_rows, width)
    d_blocks = d_all.reshape(blocks, block_rows, width)
    ok_blocks = row_ok_all.reshape(blocks, block_rows)

    def stat_block(carry, items):
        q_rows, d_rows, ok_rows = items
        allowed = ok_rows[:, None] & key_ok[None, :]
        return (carry, block_stats(q_rows, d_rows, k_b, values, kv_heads, allowed))

    _, (t_blocks, w_blocks) = lax.scan(
        stat_block, jnp.float32(0.0), (q_blocks, d_blocks, ok_blocks)
    )
    totals = t_blocks.transpose(1, 0, 2).reshape(q_heads, every)
    weighted = w_blocks.transpose(1, 0, 2).reshape(q_heads, every)
    totals, weighted = in_one((totals, weighted), "frame")
    t_blocks = totals.reshape(q_heads, blocks, block_rows).transpose(1, 0, 2)
    w_blocks = weighted.reshape(q_heads, blocks, block_rows).transpose(1, 0, 2)

    def grad_block(carry, items):
        dk_cur, dv_cur = carry
        q_rows, d_rows, ok_rows, t_rows, w_rows = items
        allowed = ok_rows[:, None] & key_ok[None, :]
        dq_part, dk_part, dv_part = block_grads(
            q_rows, d_rows, k_b, values, kv_heads, allowed, t_rows, w_rows
        )
        return ((dk_cur + dk_part, dv_cur + dv_part), dq_part)

    (dk_acc, dv_acc), dq_blocks = lax.scan(
        grad_block, (zero_kv, zero_kv), (q_blocks, d_blocks, ok_blocks, t_blocks, w_blocks)
    )
    dq_total = summed_on_arrival(dq_blocks.reshape(every, width).astype(jnp.bfloat16), "frame", 0)
    grad_q = dq_total.reshape(rows, q_heads, head_size) * head_size ** (-0.5) * q_gain
    dq_raw = norm_bwd(q_raw, q_scale, grad_q).reshape(rows, width).astype(jnp.bfloat16)
    text_term = lax.dot_general(
        dq_raw, w_query, (((1,), (1,)), ((), ())), preferred_element_type=jnp.float32
    )
    text_grad = summed_on_arrival(text_term.astype(jnp.bfloat16), "head", 1)
    grad_k = dk_acc * k_gain
    key_grad = norm_bwd(k_raw, k_scale, grad_k).reshape(key_rows, kv_heads * head_size)
    value_grad = dv_acc.reshape(key_rows, kv_heads * head_size)
    return (text_grad, key_grad, value_grad)


def solution(mesh):
    return jax.shard_map(
        local,
        mesh=mesh,
        in_specs=(
            P("frame", "head"),
            P(),
            P("frame", "head"),
            P(),
            P("frame", "head"),
            P("frame", "head"),
            P(None, "head"),
            P(None, "frame"),
            P("frame"),
        ),
        out_specs=(P("frame", "head"), P("frame", "head"), P("frame", "head")),
        check_vma=False,
    )
```

profile of v0, /device:TPU:1, one launch (start us, length us, event | category | flops | bytes accessed | tf_op | source)
XLA Modules:
  0.0 257.6 jit_solution(9018556940210782676)
XLA Ops:
  17.1 36.6 %all-gather.2.cloned.1.call-done = bf16[1024,2048]{1,0:T(8,128)(2,1)} async-done(((bf16[64,2048]{1,0:T(8,128)(2,1)}), bf16[1024,2048]{1,0:T(8,128)(2,1)}) %all-gather.2.cloned.1.call-update) | async-done | bytes 4194320 | tf_op jit(solution)/shard_map/all_gather | solution.py:18
  53.7 4.0 %fusion.54 = (bf16[1024,1024]{1,0:T(8,128)(2,1)}, bf16[1024,1024]{1,0:T(8,128)(2,1)S(1)}) fusion(bf16[1024,2048]{1,0:T(8,128)(2,1)} %all-gather.2.cloned.1.call-done), kind=kLoop, calls=%fused_computation.102 | loop fusion | bytes 8388608 | tf_op jit(solution)/shard_map/split | solution.py:18
  57.7 4.0 %copy.77 = bf16[4,256,1024]{1,2,0:T(8,128)(2,1)} copy(bf16[4,256,1024]{2,1,0:T(8,128)(2,1)} %bitcast.260) | data formatting | bytes 4194304
  61.6 2.6 copy.81
  64.2 33.5 %while.28 = (s32[]{:T(128)}, f32[4,8,256]{2,1,0:T(8,128)S(1)}, f32[4,8,256]{2,1,0:T(8,128)S(1)}, pred[4,256]{1,0:T(4,128)(4,1)S(1)}, bf16[4,256,1024]{1,2,0:T(8,...) while((s32[]{:T(128)}, f32[4,8,256]{2,1,0:T(8,128)S(1)}, ...), condition=%wide.region_6.7_spmd.clone, body=%wide.region_3.6_spmd.clone.sunk | while | flops 1694512640 | bytes 31461376 | solution.py:138
  67.3 2.4 fusion.89
  69.7 2.8 %fusion.90 = f32[8,256]{1,0:T(8,128)S(1)} fusion(f32[256,8,1600]{0,2,1:T(8,128)S(1)} %get-tuple-element.461, pred[256,1600]{0,1:T(8,128)(4,1)S(1)} %broadcast_and_fusion.4, bf16[256,8,128]{0,2,1:T(8,128)(2,1)S(1)} %bitcast.258, bf16[1600,128]{1,0:T(8,128)(2,1)S(1)} %get-tuple-element.508), kind=kOutput, calls=%fused_computation.3.clone.1 | convolution fusion | flops 848689152 | bytes 14458880 | tf_op jit(solution)/shard_map/while/body/eval_jaxpr/rkgd,nkd->kgrn/dot_general | solution.py:75
  75.7 2.4 fusion.89
  78.1 2.8 %fusion.90 = f32[8,256]{1,0:T(8,128)S(1)} fusion(f32[256,8,1600]{0,2,1:T(8,128)S(1)} %get-tuple-element.461, pred[256,1600]{0,1:T(8,128)(4,1)S(1)} %broadcast_and_fusion.4, bf16[256,8,128]{0,2,1:T(8,128)(2,1)S(1)} %bitcast.258, bf16[1600,128]{1,0:T(8,128)(2,1)S(1)} %get-tuple-element.508), kind=kOutput, calls=%fused_computation.3.clone.1 | convolution fusion | flops 848689152 | bytes 14458880 | tf_op jit(solution)/shard_map/while/body/eval_jaxpr/rkgd,nkd->kgrn/dot_general | solution.py:75
  84.1 2.4 fusion.89
  86.5 2.8 %fusion.90 = f32[8,256]{1,0:T(8,128)S(1)} fusion(f32[256,8,1600]{0,2,1:T(8,128)S(1)} %get-tuple-element.461, pred[256,1600]{0,1:T(8,128)(4,1)S(1)} %broadcast_and_fusion.4, bf16[256,8,128]{0,2,1:T(8,128)(2,1)S(1)} %bitcast.258, bf16[1600,128]{1,0:T(8,128)(2,1)S(1)} %get-tuple-element.508), kind=kOutput, calls=%fused_computation.3.clone.1 | convolution fusion | flops 848689152 | bytes 14458880 | tf_op jit(solution)/shard_map/while/body/eval_jaxpr/rkgd,nkd->kgrn/dot_general | solution.py:75
  92.5 2.4 fusion.89
  94.9 2.8 %fusion.90 = f32[8,256]{1,0:T(8,128)S(1)} fusion(f32[256,8,1600]{0,2,1:T(8,128)S(1)} %get-tuple-element.461, pred[256,1600]{0,1:T(8,128)(4,1)S(1)} %broadcast_and_fusion.4, bf16[256,8,128]{0,2,1:T(8,128)(2,1)S(1)} %bitcast.258, bf16[1600,128]{1,0:T(8,128)(2,1)S(1)} %get-tuple-element.508), kind=kOutput, calls=%fused_computation.3.clone.1 | convolution fusion | flops 848689152 | bytes 14458880 | tf_op jit(solution)/shard_map/while/body/eval_jaxpr/rkgd,nkd->kgrn/dot_general | solution.py:75
  99.7 4.5 %all-to-all-start = ((f32[16,1,16384]{2,1,0:T(1,128)}), f32[16,1,16384]{2,1,0:T(1,128)S(1)}, u32[]{:S(2)}, u32[]{:S(2)}) async-start(f32[16,1,16384]{2,1,0:T(1,128)} %broadcast_in_dim.54), calls=%async_computation | async-start | bytes 2097152 | tf_op jit(solution)/shard_map/all_to_all | solution.py:23
  104.2 15.8 %all-to-all-done = f32[16,1,16384]{2,1,0:T(1,128)S(1)} async-done(((f32[16,1,16384]{2,1,0:T(1,128)}), f32[16,1,16384]{2,1,0:T(1,128)S(1)}, u32[]{:S(2)}, u32[]{:S(2)}) %all-to-all-start) | async-done | bytes 1048608 | tf_op jit(solution)/shard_map/all_to_all | solution.py:23
  120.8 60.3 %while.29 = (s32[]{:T(128)}, f32[1600,1,128]{2,0,1:T(8,128)S(1)}, f32[1600,1,128]{2,0,1:T(8,128)}, bf16[4,256,1024]{2,1,0:T(8,128)(2,1)}, bf16[4,256,1024]{1,2,0...) while((s32[]{:T(128)}, f32[1600,1,128]{2,0,1:T(8,128)S(1)}, ...), condition=%wide.region_9.10_spmd.clone, body=%wide.region_8.9_spmd.clone.sunk | while | flops 4221750784 | bytes 78188648 | solution.py:156
  125.0 2.7 %fusion.105 = f32[1600,1,128]{2,0,1:T(8,128)S(1)} fusion(bf16[256,8,128]{0,2,1:T(8,128)(2,1)S(1)} %bitcast.255, f32[8,256]{1,0:T(8,128)S(1)} %bitcast.270, f32[256,8,1600]{0,2,1:T(8,128)S(1)} %fusion.102, pred[256,1600]{0,1:T(8,128)(4,1)S(1)} %broadcast_and_fusion.5, f32[1600,1,128]{2,0,1:T(8,128)S(1)} %copy-done.12, pred[]{:T(512)S(6)} %compare.7), kind=kOutput, calls=%fused_computation.27.clone.1 | convolution fusion | flops 849100800 | bytes 15687681 | tf_op jit(solution)/shard_map/while/body/eval_jaxpr/kgrn,rkgd->nkd/dot_general | solution.py:99
  127.6 3.9 %fusion.103 = bf16[8,256,1600]{1,2,0:T(8,128)(2,1)S(1)} fusion(f32[8,256]{1,0:T(8,128)S(1)} %fusion.101, f32[8,256]{1,0:T(8,128)S(1)} %bitcast.271, f32[256,8,1600]{0,2,1:T(8,128)S(1)} %fusion.102, pred[256,1600]{0,1:T(8,128)(4,1)S(1)} %broadcast_and_fusion.5, bf16[256,8,128]{0,2,1:T(8,128)(2,1)S(1)} %bitcast.256, ...), kind=kOutput, calls=%fused_computation.21.clone.1 | convolution fusion | flops 855244800 | bytes 21020672 | tf_op jit(solution)/shard_map/while/body/eval_jaxpr/rkgd,nkd->kgrn/dot_general | solution.py:75
  131.6 2.0 fusion.104
  140.0 2.7 %fusion.105 = f32[1600,1,128]{2,0,1:T(8,128)S(1)} fusion(bf16[256,8,128]{0,2,1:T(8,128)(2,1)S(1)} %bitcast.255, f32[8,256]{1,0:T(8,128)S(1)} %bitcast.270, f32[256,8,1600]{0,2,1:T(8,128)S(1)} %fusion.102, pred[256,1600]{0,1:T(8,128)(4,1)S(1)} %broadcast_and_fusion.5, f32[1600,1,128]{2,0,1:T(8,128)S(1)} %copy-done.12, pred[]{:T(512)S(6)} %compare.7), kind=kOutput, calls=%fused_computation.27.clone.1 | convolution fusion | flops 849100800 | bytes 15687681 | tf_op jit(solution)/shard_map/while/body/eval_jaxpr/kgrn,rkgd->nkd/dot_general | solution.py:99
  142.7 3.9 %fusion.103 = bf16[8,256,1600]{1,2,0:T(8,128)(2,1)S(1)} fusion(f32[8,256]{1,0:T(8,128)S(1)} %fusion.101, f32[8,256]{1,0:T(8,128)S(1)} %bitcast.271, f32[256,8,1600]{0,2,1:T(8,128)S(1)} %fusion.102, pred[256,1600]{0,1:T(8,128)(4,1)S(1)} %broadcast_and_fusion.5, bf16[256,8,128]{0,2,1:T(8,128)(2,1)S(1)} %bitcast.256, ...), kind=kOutput, calls=%fused_computation.21.clone.1 | convolution fusion | flops 855244800 | bytes 21020672 | tf_op jit(solution)/shard_map/while/body/eval_jaxpr/rkgd,nkd->kgrn/dot_general | solution.py:75
  146.6 2.0 fusion.104
  155.1 2.7 %fusion.105 = f32[1600,1,128]{2,0,1:T(8,128)S(1)} fusion(bf16[256,8,128]{0,2,1:T(8,128)(2,1)S(1)} %bitcast.255, f32[8,256]{1,0:T(8,128)S(1)} %bitcast.270, f32[256,8,1600]{0,2,1:T(8,128)S(1)} %fusion.102, pred[256,1600]{0,1:T(8,128)(4,1)S(1)} %broadcast_and_fusion.5, f32[1600,1,128]{2,0,1:T(8,128)S(1)} %copy-done.12, pred[]{:T(512)S(6)} %compare.7), kind=kOutput, calls=%fused_computation.27.clone.1 | convolution fusion | flops 849100800 | bytes 15687681 | tf_op jit(solution)/shard_map/while/body/eval_jaxpr/kgrn,rkgd->nkd/dot_general | solution.py:99
  157.8 3.9 %fusion.103 = bf16[8,256,1600]{1,2,0:T(8,128)(2,1)S(1)} fusion(f32[8,256]{1,0:T(8,128)S(1)} %fusion.101, f32[8,256]{1,0:T(8,128)S(1)} %bitcast.271, f32[256,8,1600]{0,2,1:T(8,128)S(1)} %fusion.102, pred[256,1600]{0,1:T(8,128)(4,1)S(1)} %broadcast_and_fusion.5, bf16[256,8,128]{0,2,1:T(8,128)(2,1)S(1)} %bitcast.256, ...), kind=kOutput, calls=%fused_computation.21.clone.1 | convolution fusion | flops 855244800 | bytes 21020672 | tf_op jit(solution)/shard_map/while/body/eval_jaxpr/rkgd,nkd->kgrn/dot_general | solution.py:75
  170.2 2.7 %fusion.105 = f32[1600,1,128]{2,0,1:T(8,128)S(1)} fusion(bf16[256,8,128]{0,2,1:T(8,128)(2,1)S(1)} %bitcast.255, f32[8,256]{1,0:T(8,128)S(1)} %bitcast.270, f32[256,8,1600]{0,2,1:T(8,128)S(1)} %fusion.102, pred[256,1600]{0,1:T(8,128)(4,1)S(1)} %broadcast_and_fusion.5, f32[1600,1,128]{2,0,1:T(8,128)S(1)} %copy-done.12, pred[]{:T(512)S(6)} %compare.7), kind=kOutput, calls=%fused_computation.27.clone.1 | convolution fusion | flops 849100800 | bytes 15687681 | tf_op jit(solution)/shard_map/while/body/eval_jaxpr/kgrn,rkgd->nkd/dot_general | solution.py:99
  172.9 3.9 %fusion.103 = bf16[8,256,1600]{1,2,0:T(8,128)(2,1)S(1)} fusion(f32[8,256]{1,0:T(8,128)S(1)} %fusion.101, f32[8,256]{1,0:T(8,128)S(1)} %bitcast.271, f32[256,8,1600]{0,2,1:T(8,128)S(1)} %fusion.102, pred[256,1600]{0,1:T(8,128)(4,1)S(1)} %broadcast_and_fusion.5, bf16[256,8,128]{0,2,1:T(8,128)(2,1)S(1)} %bitcast.256, ...), kind=kOutput, calls=%fused_computation.21.clone.1 | convolution fusion | flops 855244800 | bytes 21020672 | tf_op jit(solution)/shard_map/while/body/eval_jaxpr/rkgd,nkd->kgrn/dot_general | solution.py:75
  176.8 2.0 fusion.104
  181.1 4.5 %all-to-all-start.1 = ((bf16[16,64,1024]{2,1,0:T(8,128)(2,1)}), bf16[16,64,1024]{2,1,0:T(8,128)(2,1)S(1)}, u32[]{:S(2)}, u32[]{:S(2)}) async-start(bf16[16,64,1024]{2,1,0:T(8,128)(2,1)} %bitcast.267), calls=%async_computation.1 | async-start | bytes 4194304 | tf_op jit(solution)/shard_map/all_to_all | solution.py:45
  185.6 28.1 %all-to-all-done.1 = bf16[16,64,1024]{2,1,0:T(8,128)(2,1)S(1)} async-done(((bf16[16,64,1024]{2,1,0:T(8,128)(2,1)}), bf16[16,64,1024]{2,1,0:T(8,128)(2,1)S(1)}, u32[]{:S(2)}, u32[]{:S(2)}) %all-to-all-start.1) | async-done | bytes 2097184 | tf_op jit(solution)/shard_map/all_to_all | solution.py:45
  215.7 11.2 %convolution_convert_fusion = bf16[64,8192]{1,0:T(8,128)(2,1)S(1)} fusion(bf16[8192,1024]{1,0:T(8,128)(2,1)} %param.19, bf16[64,1024]{1,0:T(8,128)(2,1)S(1)} %copy-done.4, f32[8,8,8,128]{3,2,1,0:T(8,128)S(1)} %bitcast.269, f32[8,8,8,128]{3,2,1,0:T(8,128)S(1)} %bitcast.268, f32[64,1024]{1,0:T(8,128)} %copy-done.1, f32[8,8,8,128]{3,2,1,0:T(8,128)} %bitcast.264, ...), kind=kOutput, calls=%fused_computation.46 | convolution fusion | flops 1074724864 | bytes 19009536 | tf_op jit(solution)/shard_map/dot_general | solution.py:162
  228.0 6.1 %all-to-all-start.2 = ((bf16[8,64,1024]{2,1,0:T(8,128)(2,1)}), bf16[8,64,1024]{2,1,0:T(8,128)(2,1)S(1)}, u32[]{:S(2)}, u32[]{:S(2)}) async-start(bf16[8,64,1024]{2,1,0:T(8,128)(2,1)} %bitcast.185), calls=%async_computation.2 | async-start | bytes 2097152 | tf_op jit(solution)/shard_map/all_to_all | solution.py:45
  236.3 13.6 %all-to-all-done.2 = bf16[8,64,1024]{2,1,0:T(8,128)(2,1)S(1)} async-done(((bf16[8,64,1024]{2,1,0:T(8,128)(2,1)}), bf16[8,64,1024]{2,1,0:T(8,128)(2,1)S(1)}, u32[]{:S(2)}, u32[]{:S(2)}) %all-to-all-start.2) | async-done | bytes 1048608 | tf_op jit(solution)/shard_map/all_to_all | solution.py:45
  (155 shorter events, 58.4 us)
Async XLA Ops:
  7.2 46.5 %all-gather.2.cloned.1.call-start = ((), (), s32[]{:S(2)}) async-start(), calls=%async_computation.3 | async-start | bytes 4456448 | tf_op jit(solution)/shard_map/all_gather | solution.py:18
  8.9 0.8 copy-start.3
  9.8 5.5 %copy-start.2 = (f32[64,8,128]{2,1,0:T(8,128)}, f32[64,8,128]{2,1,0:T(8,128)S(1)}, u32[]{:S(2)}) copy-start(f32[64,8,128]{2,1,0:T(8,128)S(1)} %mul.153) | copy-start | bytes 786436
  15.2 0.6 copy-start.6
  17.1 47.1 %copy-start.11 = (bf16[1600,128]{1,0:T(8,128)(2,1)S(1)}, bf16[1600,128]{1,0:T(8,128)(2,1)}, u32[]{:S(2)}) copy-start(bf16[1600,128]{1,0:T(8,128)(2,1)} %param.17) | copy-start | bytes 1228804
  99.7 20.3 %all-to-all-start = ((f32[16,1,16384]{2,1,0:T(1,128)}), f32[16,1,16384]{2,1,0:T(1,128)S(1)}, u32[]{:S(2)}, u32[]{:S(2)}) async-start(f32[16,1,16384]{2,1,0:T(1,128)} %broadcast_in_dim.54), calls=%async_computation | async-start | bytes 2097152 | tf_op jit(solution)/shard_map/all_to_all | solution.py:23
  120.8 64.8 %copy-start.10 = (f32[128]{0:T(128)S(1)}, f32[128]{0:T(128)}, u32[]{:S(2)}) copy-start(f32[128]{0:T(128)} %param.14) | copy-start | bytes 1540
  123.1 1.9 copy-start.12
  127.6 3.9 %copy-start.13 = (f32[1600,1,128]{2,0,1:T(8,128)}, f32[1600,1,128]{2,0,1:T(8,128)S(1)}, u32[]{:S(2)}) copy-start(f32[1600,1,128]{2,0,1:T(8,128)S(1)} %fusion.105) | copy-start | bytes 2457604 | tf_op jit(solution)/shard_map/while
  138.1 1.9 copy-start.12
  142.7 3.9 %copy-start.13 = (f32[1600,1,128]{2,0,1:T(8,128)}, f32[1600,1,128]{2,0,1:T(8,128)S(1)}, u32[]{:S(2)}) copy-start(f32[1600,1,128]{2,0,1:T(8,128)S(1)} %fusion.105) | copy-start | bytes 2457604 | tf_op jit(solution)/shard_map/while
  153.2 1.9 copy-start.12
  157.8 3.9 %copy-start.13 = (f32[1600,1,128]{2,0,1:T(8,128)}, f32[1600,1,128]{2,0,1:T(8,128)S(1)}, u32[]{:S(2)}) copy-start(f32[1600,1,128]{2,0,1:T(8,128)S(1)} %fusion.105) | copy-start | bytes 2457604 | tf_op jit(solution)/shard_map/while
  168.3 1.9 copy-start.12
  172.8 3.9 %copy-start.13 = (f32[1600,1,128]{2,0,1:T(8,128)}, f32[1600,1,128]{2,0,1:T(8,128)S(1)}, u32[]{:S(2)}) copy-start(f32[1600,1,128]{2,0,1:T(8,128)S(1)} %fusion.105) | copy-start | bytes 2457604 | tf_op jit(solution)/shard_map/while
  181.1 34.3 %copy-start.5 = (f32[64,8]{1,0:T(8,128)S(1)}, f32[64,8]{1,0:T(8,128)}, u32[]{:S(2)}) copy-start(f32[64,8]{1,0:T(8,128)} %get-tuple-element.333) | copy-start | bytes 6148
  181.1 34.6 %copy-start.4 = (bf16[64,1024]{1,0:T(8,128)(2,1)S(1)}, bf16[64,1024]{1,0:T(8,128)(2,1)}, u32[]{:S(2)}) copy-start(bf16[64,1024]{1,0:T(8,128)(2,1)} %param.13) | copy-start | bytes 393220
  181.1 32.7 %all-to-all-start.1 = ((bf16[16,64,1024]{2,1,0:T(8,128)(2,1)}), bf16[16,64,1024]{2,1,0:T(8,128)(2,1)S(1)}, u32[]{:S(2)}, u32[]{:S(2)}) async-start(bf16[16,64,1024]{2,1,0:T(8,128)(2,1)} %bitcast.267), calls=%async_computation.1 | async-start | bytes 4194304 | tf_op jit(solution)/shard_map/all_to_all | solution.py:45
  214.1 1.5 copy-start.1
  215.6 18.4 %copy-start = (bf16[1600,128]{1,0:T(8,128)(2,1)S(1)}, bf16[1600,128]{1,0:T(8,128)(2,1)}, u32[]{:S(2)}) copy-start(bf16[1600,128]{1,0:T(8,128)(2,1)} %param.15) | copy-start | bytes 1228804
  215.7 18.4 %copy-start.9 = (f32[128]{0:T(128)S(1)}, f32[128]{0:T(128)}, u32[]{:S(2)}) copy-start(f32[128]{0:T(128)} %param.16) | copy-start | bytes 1540
  215.7 18.8 %copy-start.7 = (f32[1600]{0:T(1024)S(1)}, f32[1600]{0:T(1024)}, u32[]{:S(2)}) copy-start(f32[1600]{0:T(1024)} %copy-done.6) | copy-start | bytes 19204
  215.7 18.8 %copy-start.8 = (f32[1600]{0:T(1024)S(1)}, f32[1600]{0:T(1024)}, u32[]{:S(2)}) copy-start(f32[1600]{0:T(1024)} %get-tuple-element.335) | copy-start | bytes 19204
  228.0 21.9 %all-to-all-start.2 = ((bf16[8,64,1024]{2,1,0:T(8,128)(2,1)}), bf16[8,64,1024]{2,1,0:T(8,128)(2,1)S(1)}, u32[]{:S(2)}, u32[]{:S(2)}) async-start(bf16[8,64,1024]{2,1,0:T(8,128)(2,1)} %bitcast.185), calls=%async_computation.2 | async-start | bytes 2097152 | tf_op jit(solution)/shard_map/all_to_all | solution.py:45
Sparse Core Ops, SparseCore 0:
  12.6 41.0 all-gather.1
where the time goes:
time: 260 us; the launch traced here: 258 us
  waiting for transfers between devices  94.1 us (36%)
  matrix products  78.5 us (30%)
  local copies, waits for them, and re-layouts  33.7 us (13%)
  other arithmetic  21.1 us (8%)
  starting transfers between devices  15.2 us (6%)
  between operations  14.4 us (6%)
    all_to_all x2, waiting for transfers between devices, summed_on_arrival(): lax.all_to_all(parts, axis, split_axis=0, concat_axis=0, tiled=True)  41.7 us
    all_gather x1, waiting for transfers between devices, sent_together(): lax.all_gather(both, axis, axis=dim, tiled=True)  36.6 us
    dot_general x8, matrix products, block_scores(): jnp.einsum('rkgd,nkd->kgrn', d_heads, v_heads, preferred_element_type=jnp...  26.9 us
    dot_general x8, matrix products, block_scores(): jnp.einsum('rkgd,nkd->kgrn', q_heads, k_heads, preferred_element_type=jnp...  17 us
    all_to_all x1, waiting for transfers between devices, copy_for_each(): return lax.all_to_all(copies, axis, split_axis=0, concat_axis=0, tiled=True)  15.8 us
    dynamic_slice x20, local copies, waits for them, and re-layouts, local(): lax.scan(stat_block, jnp.float32(0.0), (q_blocks, d_blocks, ok_blocks))  14 us
    dot_general x1, matrix products, local(): lax.dot_general(dq_raw, w_query, (((1,), (1,)), ((), ())), preferred_elem...  11.2 us
    dot_general x4, matrix products, block_grads(): jnp.einsum('kgrn,rkgd->nkd', prob_b, d_heads, preferred_element_type=jnp....  10.6 us
  transfers between devices with their start and end apart: 4, of which 4 were waited for; matrix products, arithmetic and copies ran while one was open for 2% of the time, Pallas kernels for 0%

commit v1 on v0

v1 whole, which is shorter than its diff:
```python
import functools

import jax
import jax.numpy as jnp
from jax import lax
from jax.experimental import pallas as pl
from jax.experimental.pallas import tpu as pltpu
from jax.sharding import PartitionSpec as P

MESH = pl.DeviceIdType.MESH
BLK = 16
EPS = 1e-05
HD = 128
LAG = 2
SLOTS = LAG + 1
CHUNK = 320
F32 = jnp.float32
BF16 = jnp.bfloat16
NT = (((1,), (1,)), ((), ()))


def attention_kernel(
    heads, chips, rows, q_ref, qg_ref, k_ref, kg_ref, v_ref, d_ref, span_ref, len_ref,
    dq_ref, dk_ref, dv_ref,
    qd, e_buf, f_buf, kb, kt, km, rm, lu, lu_sib, lu_chip, lu_all, dq_part, dq_sib, dq_chip, dq_all,
    ag_send, ag_recv, fw_send, fw_recv, s1_send, s1_recv, s2_send, s2_recv,
    r1_send, r1_recv, r2_send, r2_recv,
):
    me = lax.axis_index("frame")
    core = lax.rem(me, 2)
    chip = me // 2
    sibling = me + 1 - 2 * core
    half = chips * rows
    every = 2 * half
    keys = k_ref.shape[0]
    peers = chips - 1

    def peer(k):
        return 2 * lax.rem(chip + k, chips) + core

    def push(src, dst, send, recv, target):
        return pltpu.make_async_remote_copy(
            src_ref=src, dst_ref=dst, send_sem=send, recv_sem=recv,
            device_id={"frame": target}, device_id_type=MESH,
        )

    barrier = pltpu.get_barrier_semaphore()
    pl.semaphore_signal(barrier, inc=1, device_id={"frame": sibling}, device_id_type=MESH)
    for k in range(1, chips):
        pl.semaphore_signal(barrier, inc=1, device_id={"frame": peer(k)}, device_id_type=MESH)

    mine = pl.multiple_of(core * half + chip * rows, rows)
    for h in range(heads):
        at = slice(h * HD, (h + 1) * HD)
        q = q_ref[:, at].astype(F32)
        scale = lax.rsqrt(jnp.mean(q * q, axis=-1, keepdims=True) + EPS)
        qd[h, pl.ds(mine, rows), :HD] = (q * scale * qg_ref[...] * HD ** (-0.5)).astype(BF16)
        qd[h, pl.ds(mine, rows), HD:] = d_ref[:, at]
    pl.semaphore_wait(barrier, chips)

    def gather_copy(h, k):
        block = qd.at[h, pl.ds(mine, rows)]
        return push(block, block, ag_send.at[h], ag_recv.at[h], peer(k))

    def gather_all(h):
        block = qd.at[h, pl.ds(0, peers * rows)]
        return push(block, block, ag_send.at[h], ag_recv.at[h], sibling)

    def forward(h):
        block = qd.at[h, pl.ds(pl.multiple_of(core * half, half), half)]
        return push(block, block, fw_send.at[h], fw_recv.at[h], sibling)

    def send_block(h, carry):
        for k in range(1, chips):
            gather_copy(h, k).start()
        return carry

    lax.fori_loop(0, heads, send_block, 0)

    k = k_ref[...].astype(F32)
    scale = lax.rsqrt(jnp.mean(k * k, axis=-1, keepdims=True) + EPS)
    k = k * scale * kg_ref[...]
    kb[...] = k.astype(BF16)
    kt[...] = k.T.astype(BF16)
    km[...] = (lax.broadcasted_iota(jnp.int32, km.shape, 0) < len_ref[0]).astype(F32)
    r = lax.broadcasted_iota(jnp.int32, (span_ref.shape[0], every), 1)
    owner = 2 * ((r % half) // rows) + r // half
    span_of = owner * (rows // BLK) + (r % rows) // BLK
    hit = span_of == lax.broadcasted_iota(jnp.int32, r.shape, 0)
    rm[...] = jnp.sum(jnp.where(hit & (span_ref[...] > 0), 1.0, 0.0), axis=0, keepdims=True)
    dk_ref[...] = jnp.zeros_like(dk_ref)
    dv_ref[...] = jnp.zeros_like(dv_ref)

    def stat_sib(h):
        return push(lu.at[h], lu_sib.at[h], s1_send.at[h], s1_recv.at[h], sibling)

    def stat_copy(h, k):
        return push(lu_chip.at[h], lu_all.at[h, chip], s2_send.at[h], s2_recv.at[h], peer(k))

    def stat_all(h):
        block = lu_all.at[h, pl.ds(0, peers)]
        return push(block, block, s2_send.at[h], s2_recv.at[h], sibling)

    def dq_to_sib(h):
        return push(
            dq_part.at[h, pl.ds(pl.multiple_of((1 - core) * half, half), half)], dq_sib.at[h],
            r1_send.at[h], r1_recv.at[h], sibling,
        )

    def dq_copy(h, k):
        to = lax.rem(chip + k, chips)
        return push(
            dq_chip.at[h, pl.ds(pl.multiple_of(to * rows, rows), rows)], dq_all.at[h, chip],
            r2_send.at[h], r2_recv.at[h], peer(k),
        )

    def dq_all_of(h):
        block = dq_all.at[h, pl.ds(0, peers)]
        return push(block, block, r2_send.at[h], r2_recv.at[h], sibling)

    def first_pass(h):
        slot = lax.rem(h, SLOTS)
        q, d = qd[h, :, :HD], qd[h, :, HD:]
        l = jnp.zeros((1, every), F32)
        u = jnp.zeros((1, every), F32)
        for m in range(0, keys, CHUNK):
            s = lax.dot_general(kb[m : m + CHUNK], q, NT, preferred_element_type=F32)
            dp = lax.dot_general(v_ref[m : m + CHUNK], d, NT, preferred_element_type=F32)
            live = jnp.concatenate([km[m : m + CHUNK]] * (every // HD), axis=1)
            e = jnp.exp(s) * live
            f = e * dp
            e_buf[slot, m : m + CHUNK] = e.astype(BF16)
            f_buf[slot, m : m + CHUNK] = f.astype(BF16)
            l += jnp.sum(e, axis=0, keepdims=True)
            u += jnp.sum(f, axis=0, keepdims=True)
        l *= rm[...]
        u *= rm[...]
        n = every // HD
        for i in range(n):
            lu[h, i : i + 1] = l[:, i * HD : (i + 1) * HD]
            lu[h, n + i : n + i + 1] = u[:, i * HD : (i + 1) * HD]

    def second_pass(h):
        slot = lax.rem(h, SLOTS)
        q, d = qd[h, :, :HD], qd[h, :, HD:]
        total = lu_all[h, 0]
        for c in range(1, chips):
            total = total + lu_all[h, c]
        n = every // HD
        l = jnp.concatenate([total[i : i + 1] for i in range(n)], axis=1)
        u = jnp.concatenate([total[n + i : n + i + 1] for i in range(n)], axis=1)
        il = rm[...] / l
        w = (u / l) * il
        col = jnp.concatenate([il] * 8, axis=0).T[:, 0:1]
        x = (d.astype(F32) * col).astype(BF16)
        for m in range(0, keys, CHUNK):
            e = e_buf[slot, m : m + CHUNK]
            f = f_buf[slot, m : m + CHUNK]
            ds = (f.astype(F32) * il - e.astype(F32) * w).astype(BF16)
            f_buf[slot, m : m + CHUNK] = ds
            dv_ref[m : m + CHUNK] += jnp.dot(e, x, preferred_element_type=F32)
            dk_ref[m : m + CHUNK] += jnp.dot(ds, q, preferred_element_type=F32)
        dqt = jnp.dot(kt[...], f_buf[slot], preferred_element_type=F32)
        dq_part[h] = dqt.T.astype(BF16)

    def second_dq(h):
        dq_to_sib(h).wait_recv()
        own = dq_part[h, pl.ds(pl.multiple_of(core * half, half), half)]
        dq_chip[h] = (own.astype(F32) + dq_sib[h].astype(F32)).astype(BF16)
        dq_all[h, chip] = dq_chip[h, pl.ds(pl.multiple_of(chip * rows, rows), rows)]
        for k in range(1, chips):
            dq_copy(h, k).start()

    gather_all(0).wait_recv()
    forward(0).start()

    def step(s, carry):
        @pl.when(s + 1 < heads)
        def _():
            gather_all(s + 1).wait_recv()
            forward(s + 1).start()

        @pl.when(s < heads)
        def _():
            forward(s).wait_recv()
            first_pass(s)
            stat_sib(s).start()

        @pl.when(s > LAG)
        def _():
            second_dq(s - LAG - 1)

        @pl.when(s >= LAG)
        def _():
            stat_all(s - LAG).wait_recv()
            second_pass(s - LAG)
            dq_to_sib(s - LAG).start()

        @pl.when(s < heads)
        def _():
            stat_sib(s).wait_recv()
            both = lu[s] + lu_sib[s]
            lu_chip[s] = both
            lu_all[s, chip] = both
            for k in range(1, chips):
                stat_copy(s, k).start()

        return carry

    lax.fori_loop(0, heads + LAG, step, 0)
    second_dq(heads - 1)

    def drain(h, carry):
        gather_all(h).wait_send()
        forward(h).wait_send()
        stat_sib(h).wait_send()
        stat_all(h).wait_send()
        dq_to_sib(h).wait_send()
        dq_all_of(h).wait_send()
        return carry

    for h in range(heads):
        dq_all_of(h).wait_recv()
        total = dq_all[h, 0].astype(F32)
        for c in range(1, chips):
            total = total + dq_all[h, c].astype(F32)
        at = slice(h * HD, (h + 1) * HD)
        q = q_ref[:, at].astype(F32)
        scale = lax.rsqrt(jnp.mean(q * q, axis=-1, keepdims=True) + EPS)
        g = total * HD ** (-0.5) * qg_ref[...]
        dq = scale * g - q * scale**3 * jnp.mean(q * g, axis=-1, keepdims=True)
        dq_ref[:, at] = dq.astype(BF16)
    lax.fori_loop(0, heads, drain, 0)


def attention(queries, q_gain, keys, k_gain, values, out_grad, span_col, frame_len):
    rows, width = queries.shape
    heads = width // HD
    chips = lax.axis_size("frame") // 2
    every = 2 * chips * rows
    n = keys.shape[0]
    vmem = pl.BlockSpec(memory_space=pltpu.VMEM)
    smem = pl.BlockSpec(memory_space=pltpu.SMEM)
    sems = pltpu.SemaphoreType.DMA((heads,))
    stat = 2 * every // HD
    return pl.pallas_call(
        functools.partial(attention_kernel, heads, chips, rows),
        out_shape=(
            jax.ShapeDtypeStruct((rows, width), BF16),
            jax.ShapeDtypeStruct((n, HD), F32),
            jax.ShapeDtypeStruct((n, HD), F32),
        ),
        in_specs=[vmem] * 7 + [smem],
        out_specs=(vmem, vmem, vmem),
        scratch_shapes=[
            pltpu.VMEM((heads, every, 2 * HD), BF16),
            pltpu.VMEM((SLOTS, n, every), BF16),
            pltpu.VMEM((SLOTS, n, every), BF16),
            pltpu.VMEM((n, HD), BF16),
            pltpu.VMEM((HD, n), BF16),
            pltpu.VMEM((n, HD), F32),
            pltpu.VMEM((1, every), F32),
            pltpu.VMEM((heads, stat, HD), F32),
            pltpu.VMEM((heads, stat, HD), F32),
            pltpu.VMEM((heads, stat, HD), F32),
            pltpu.VMEM((heads, chips, stat, HD), F32),
            pltpu.VMEM((heads, every, HD), BF16),
            pltpu.VMEM((heads, every // 2, HD), BF16),
            pltpu.VMEM((heads, every // 2, HD), BF16),
            pltpu.VMEM((heads, chips, rows, HD), BF16),
        ] + [sems] * 12,
        compiler_params=pltpu.CompilerParams(
            collective_id=0, has_side_effects=True, vmem_limit_bytes=56 * 2**20
        ),
        cost_estimate=pl.CostEstimate(
            flops=10 * heads * every * n * HD, bytes_accessed=2**23, transcendentals=heads * every * n
        ),
    )(queries, q_gain[None], keys, k_gain[None], values, out_grad, span_col, frame_len)


def summed_on_arrival(value, axis, dim):
    before, after = value.shape[:dim], value.shape[dim + 1 :]
    parts = jnp.moveaxis(value.reshape(*before, lax.axis_size(axis), -1, *after), dim, 0)
    arrived = lax.all_to_all(parts, axis, split_axis=0, concat_axis=0, tiled=True)
    return arrived.astype(F32).sum(axis=0)


def local(queries, q_gain, keys, k_gain, values, out_grad, w_query, span_mask, frame_len):
    dq_raw, dk_acc, dv_acc = attention(
        queries, q_gain, keys, k_gain, values, out_grad, span_mask, frame_len
    )
    text_term = lax.dot_general(dq_raw, w_query, (((1,), (1,)), ((), ())), preferred_element_type=F32)
    text_grad = summed_on_arrival(text_term.astype(BF16), "head", 1)
    k_raw = keys.astype(F32)
    k_scale = lax.rsqrt(jnp.mean(k_raw * k_raw, axis=-1, keepdims=True) + EPS)
    g = dk_acc * k_gain
    key_grad = k_scale * g - k_raw * k_scale**3 * jnp.mean(k_raw * g, axis=-1, keepdims=True)
    return (text_grad, key_grad, dv_acc)


def solution(mesh):
    return jax.shard_map(
        local,
        mesh=mesh,
        in_specs=(
            P("frame", "head"), P(), P("frame", "head"), P(), P("frame", "head"),
            P("frame", "head"), P(None, "head"), P(None, "frame"), P("frame"),
        ),
        out_specs=(P("frame", "head"), P("frame", "head"), P("frame", "head")),
        check_vma=False,
    )
```

time: 260 us -> 118 us (0.45)
  waiting for transfers between devices: 94.1 us -> 14.7 us
  Pallas kernels: 0 us -> 77.5 us
  matrix products: 78.5 us -> 11.2 us
  local copies, waits for them, and re-layouts: 33.7 us -> 3.36 us
  other arithmetic: 21.1 us -> 3.23 us
  between operations: 14.4 us -> 1.36 us
  starting transfers between devices: 15.2 us -> 6.53 us
    pallas_call x0 -> x1, Pallas kernels: none -> 77.5 us  [attention(): pl.pallas_call(functools.partial(attention_kernel, heads, chips, rows), o...]
    dot_general x28 -> x0, matrix products: 67.3 us -> none  [the longest x8 26.9 us: block_scores(): jnp.einsum('rkgd,nkd->kgrn', d_heads, v_heads, preferred_element_type=jnp...]
    all_gather x1 -> x0, waiting for transfers between devices: 36.6 us -> none  [sent_together(): lax.all_gather(both, axis, axis=dim, tiled=True)]
    all_to_all x2 -> x1, waiting for transfers between devices: 41.7 us -> 14.7 us  [summed_on_arrival(): lax.all_to_all(parts, axis, split_axis=0, concat_axis=0, tiled=True)]
    all_to_all x1 -> x0, waiting for transfers between devices: 15.8 us -> none  [copy_for_each(): return lax.all_to_all(copies, axis, split_axis=0, concat_axis=0, tiled=True)]
    dynamic_slice x28 -> x0, local copies, waits for them, and re-layouts: 14.1 us -> none  [the longest x20 14 us: local(): lax.scan(stat_block, jnp.float32(0.0), (q_blocks, d_blocks, ok_blocks))]
    lt x8 -> x0, other arithmetic: 5.2 us -> none  [local(): key_ok = jnp.arange(key_rows, dtype=jnp.int32) < frame_len[0]]
    unnamed x30 -> x10, local copies, waits for them, and re-layouts: 7.3 us -> 2.27 us
  transfers between devices with their start and end apart: 4 -> 1, of which waited for: 4 -> 1; matrix products, arithmetic and copies ran while one was open for 2% -> 2% of each run, Pallas kernels for 0% -> 0%
where the time goes in v1:
time: 118 us
  Pallas kernels  77.5 us (66%)
  waiting for transfers between devices  14.7 us (12%)
  matrix products  11.2 us (9%)
  starting transfers between devices  6.53 us (6%)
  local copies, waits for them, and re-layouts  3.36 us (3%)
  other arithmetic  3.23 us (3%)
  between operations  1.36 us (1%)
    pallas_call x1, Pallas kernels, attention(): pl.pallas_call(functools.partial(attention_kernel, heads, chips, rows), o...  77.5 us
    all_to_all x1, waiting for transfers between devices, summed_on_arrival(): lax.all_to_all(parts, axis, split_axis=0, concat_axis=0, tiled=True)  14.7 us
    dot_general x1, matrix products, local(): lax.dot_general(dq_raw, w_query, (((1,), (1,)), ((), ())), preferred_elem...  11.2 us
    all_to_all x1, starting transfers between devices, summed_on_arrival(): lax.all_to_all(parts, axis, split_axis=0, concat_axis=0, tiled=True)  6.53 us
  transfers between devices with their start and end apart: 1, of which 1 were waited for; matrix products, arithmetic and copies ran while one was open for 2% of the time, Pallas kernels for 0%

profile of v1, /device:TPU:1, one launch (start us, length us, event | category | flops | bytes accessed | tf_op | source)
XLA Modules:
  0.0 117.8 jit_solution(225700554781540188)
XLA Ops:
  1.3 1.4 %copy.13.span_ref = s32[64,1]{1,0:T(8,128)} copy(s32[64,1]{0,1:T(1,128)} %param.16) | data formatting | bytes 512 | tf_op args[7]
  2.6 77.5 %shard_map.112 = (bf16[64,1024]{1,0:T(8,128)(2,1)}, f32[1600,128]{1,0:T(8,128)}, f32[1600,128]{1,0:T(8,128)}) custom-call(bf16[64,1024]{1,0:T(8,128)(2,1)} %q_ref.1, f32[1,128]{1,0:T(1,128)} %bitcast.13, bf16[1600,128]{1,0:T(8,128)(2,1)} %k_ref.1, f32[1,128]{1,0:T(1,128)} %bitcast.12, bf16[1600,128]{1,0:T(8,128)(2,1)} %v_ref.1, bf16[64,1024]{1,0:T(8,128)(2,1)} %d_ref.1, ...), custom_call_target="tpu_custom_call" | custom-call | flops 16777216000 | bytes 8388608 | tf_op jit(solution)/shard_map/pallas_call | solution.py:246
  80.2 0.0 copy-start
  80.2 0.0 copy-start.1
  80.2 0.0 copy-start.3
  80.2 0.0 copy-start.2
  80.2 11.2 %convolution_convert_fusion = bf16[64,8192]{1,0:T(8,128)(2,1)S(1)} fusion(bf16[64,1024]{1,0:T(8,128)(2,1)} %get-tuple-element.6, bf16[8192,1024]{1,0:T(8,128)(2,1)} %param.15), kind=kOutput, calls=%fused_computation | convolution fusion | flops 1074266112 | bytes 17956864 | tf_op jit(solution)/shard_map/dot_general | solution.py:292
  91.4 1.1 copy.17
  92.5 6.5 %all-to-all-start = ((bf16[8,64,1024]{2,1,0:T(8,128)(2,1)}), bf16[8,64,1024]{2,1,0:T(8,128)(2,1)S(1)}, u32[]{:S(2)}, u32[]{:S(2)}) async-start(bf16[8,64,1024]{2,1,0:T(8,128)(2,1)} %bitcast.10), calls=%async_computation | async-start | bytes 2097152 | tf_op jit(solution)/shard_map/all_to_all | solution.py:284
  99.0 0.0 copy-done
  99.0 0.0 copy-done.1
  99.0 0.0 copy-done.3
  99.0 0.5 fusion
  99.6 1.8 %fusion.2 = f32[1600,128]{1,0:T(8,128)} fusion(bf16[1600,128]{1,0:T(8,128)(2,1)S(1)} %copy-done.1, f32[1600,128]{1,0:T(8,128)S(1)} %copy-done, f32[1600]{0:T(1024)S(1)} %broadcast_multiply_fusion, f32[1600]{0:T(1024)S(1)} %get-tuple-element.12, f32[128]{0:T(128)S(1)} %copy-done.3, f32[1600]{0:T(1024)S(1)} %get-tuple-element.11), kind=kLoop, calls=%fused_computation.8 | loop fusion | flops 1228800 | bytes 2067712 | tf_op jit(solution)/shard_map/sub | solution.py:297
  101.4 14.7 %all-to-all-done = bf16[8,64,1024]{2,1,0:T(8,128)(2,1)S(1)} async-done(((bf16[8,64,1024]{2,1,0:T(8,128)(2,1)}), bf16[8,64,1024]{2,1,0:T(8,128)(2,1)S(1)}, u32[]{:S(2)}, u32[]{:S(2)}) %all-to-all-start) | async-done | bytes 1048608 | tf_op jit(solution)/shard_map/all_to_all | solution.py:284
  116.1 0.9 convert_reduce_fusion
  116.9 0.0 copy-done.2
  116.9 0.9 copy.20
  (2 shorter events, 0.0 us)
Async XLA Ops:
  80.2 18.8 %copy-start = (f32[1600,128]{1,0:T(8,128)S(1)}, f32[1600,128]{1,0:T(8,128)}, u32[]{:S(2)}) copy-start(f32[1600,128]{1,0:T(8,128)} %get-tuple-element.7) | copy-start | bytes 2457604
  80.2 18.8 %copy-start.1 = (bf16[1600,128]{1,0:T(8,128)(2,1)S(1)}, bf16[1600,128]{1,0:T(8,128)(2,1)}, u32[]{:S(2)}) copy-start(bf16[1600,128]{1,0:T(8,128)(2,1)} %k_ref.1) | copy-start | bytes 1228804
  80.2 18.8 %copy-start.3 = (f32[128]{0:T(128)S(1)}, f32[128]{0:T(128)}, u32[]{:S(2)}) copy-start(f32[128]{0:T(128)} %param.12) | copy-start | bytes 1540
  80.2 36.7 %copy-start.2 = (f32[1600,128]{1,0:T(8,128)S(1)}, f32[1600,128]{1,0:T(8,128)}, u32[]{:S(2)}) copy-start(f32[1600,128]{1,0:T(8,128)} %get-tuple-element.18) | copy-start | bytes 2457604
  92.5 23.6 %all-to-all-start = ((bf16[8,64,1024]{2,1,0:T(8,128)(2,1)}), bf16[8,64,1024]{2,1,0:T(8,128)(2,1)S(1)}, u32[]{:S(2)}, u32[]{:S(2)}) async-start(bf16[8,64,1024]{2,1,0:T(8,128)(2,1)} %bitcast.10), calls=%async_computation | async-start | bytes 2097152 | tf_op jit(solution)/shard_map/all_to_all | solution.py:284

commit v2 on v1

v2 whole, which is shorter than its diff:
```python
import functools

import jax
import jax.numpy as jnp
from jax import lax
from jax.experimental import pallas as pl
from jax.experimental.pallas import tpu as pltpu
from jax.sharding import PartitionSpec as P

MESH = pl.DeviceIdType.MESH
BLK = 16
EPS = 1e-05
HD = 128
LAG = 2
SLOTS = LAG + 1
CHUNK = 320
F32 = jnp.float32
BF16 = jnp.bfloat16
NT = (((1,), (1,)), ((), ()))


def kernel(
    heads, rows, q_ref, qg_ref, k_ref, kg_ref, v_ref, d_ref, span_ref, len_ref, w_ref,
    text_ref, dk_ref, dv_ref,
    qd, e_buf, f_buf, kb, kt, km, rm, dk, dv, lu, lu_in, lu_chip, lu_all, dq_part, dq_in0, dq_s0, dq_in1, dq_s1,
    dq_in2, dq, w_buf, t_out, t_in,
    ag_send, ag_recv, st_send, st_recv, rs_send, rs_recv, tx_send, tx_recv, w_sem, out_sem,
):
    frame = lax.axis_index("frame")
    head = lax.axis_index("head")
    core = lax.rem(frame, 2)
    z = lax.rem(frame // 2, 4)
    x = frame // 8
    chip = frame // 2
    half = 8 * rows
    every = 2 * half
    keys = k_ref.shape[0]
    groups = every // HD
    cols = text_ref.shape[1]

    def frame_of(x_, z_, core_):
        return {"frame": x_ * 8 + z_ * 2 + core_}

    def around(k):
        return lax.rem(z + k, 4)

    sib = frame_of(x, z, 1 - core)
    x_near = frame_of(1 - x, z, core)

    def peer(k):
        return {"frame": 2 * lax.rem(chip + k, 8) + core}

    def group(k):
        return lax.rem(head + k, 8)

    def push(src, dst, send, recv, target):
        return pltpu.make_async_remote_copy(
            src_ref=src, dst_ref=dst, send_sem=send, recv_sem=recv, device_id=target, device_id_type=MESH
        )

    def span_of_rows(first, count, size):
        return pl.ds(pl.multiple_of(first, size), count)

    barrier = pltpu.get_barrier_semaphore()
    pl.semaphore_signal(barrier, inc=1, device_id=sib, device_id_type=MESH)
    for k in range(1, 8):
        pl.semaphore_signal(barrier, inc=1, device_id=peer(k), device_id_type=MESH)
        pl.semaphore_signal(barrier, inc=1, device_id={"head": group(k)}, device_id_type=MESH)

    def index(par, x_, z_):
        return x_ * 4 + z_ if par == 0 else z_ * 2 + x_

    def gather(h, par, stage):
        if stage == 2:
            block = qd.at[h, span_of_rows(core * half, half, half)]
            return [push(block, block, ag_send.at[2, h], ag_recv.at[2, h], sib)]
        if par == 0:
            first, blocks = ((index(0, x, z), 1), (x * 4, 4))[stage]
            along_z = stage == 0
        else:
            first, blocks = ((index(1, x, z), 1), (z * 2, 2))[stage]
            along_z = stage == 1
        block = qd.at[h, span_of_rows(core * half + first * rows, blocks * rows, rows)]
        targets = [frame_of(x, around(k), core) for k in (1, 2, 3)] if along_z else [x_near]
        return [push(block, block, ag_send.at[stage, h], ag_recv.at[stage, h], t) for t in targets]

    def gather_bytes(h, par, stage):
        count = (half, (3 * rows, 4 * rows), (rows, 6 * rows))[0 if stage == 2 else 1 + par]
        count = count if stage == 2 else count[stage]
        block = qd.at[h, pl.ds(0, count)]
        return push(block, block, ag_send.at[stage, h], ag_recv.at[stage, h], sib)

    def go(copies):
        for copy in copies:
            copy.start()

    def advance(h, par, stage):
        gather_bytes(h, par, stage).wait_recv()
        go(gather(h, par, stage + 1))

    def head_rows(h):
        at = slice(h * HD, (h + 1) * HD)
        mine = span_of_rows(core * half + index(h % 2, x, z) * rows, rows, rows)
        q = q_ref[:, at].astype(F32)
        scale = lax.rsqrt(jnp.mean(q * q, axis=-1, keepdims=True) + EPS)
        qd[h, mine, :HD] = (q * scale * qg_ref[...] * HD ** (-0.5)).astype(BF16)
        qd[h, mine, HD:] = d_ref[:, at]

    def first_block(k):
        block = qd.at[0, span_of_rows(core * half + index(0, x, z) * rows, rows, rows)]
        return push(block, block, ag_send.at[0, 0], ag_recv.at[0, 0], peer(k))

    def first_bytes():
        block = qd.at[0, pl.ds(0, 7 * rows)]
        return push(block, block, ag_send.at[0, 0], ag_recv.at[0, 0], sib)

    head_rows(0)
    pl.semaphore_wait(barrier, 15)
    for k in range(1, 8):
        first_block(k).start()
    head_rows(1)
    go(gather(1, 1, 0))
    for h in range(2, heads):
        head_rows(h)
    for t in range(heads):
        pltpu.make_async_copy(w_ref.at[pl.ds(t * cols, cols)], w_buf.at[t], w_sem.at[t]).start()

    k = k_ref[...].astype(F32)
    k_scale = lax.rsqrt(jnp.mean(k * k, axis=-1, keepdims=True) + EPS)
    k = k * k_scale * kg_ref[...]
    kb[...] = k.astype(BF16)
    kt[...] = k.T.astype(BF16)
    advance(1, 1, 0)
    go(gather(2, 0, 0))
    km[...] = (lax.broadcasted_iota(jnp.int32, km.shape, 0) < len_ref[0]).astype(F32)
    spans = span_ref.shape[1]
    r = lax.broadcasted_iota(jnp.int32, (spans, every), 1)
    i = (r // rows) % 8
    for par in range(2):
        chip_of = i if par == 0 else (i % 2) * 4 + i // 2
        span_of = (chip_of * 2 + r // half) * (rows // BLK) + (r % rows) // BLK
        hit = (span_of == lax.broadcasted_iota(jnp.int32, r.shape, 0)).astype(F32)
        seen = jnp.broadcast_to((span_ref[...] > 0).astype(F32), (8, spans))
        rm[par] = jnp.dot(seen, hit, preferred_element_type=F32)[0:1]
    dk[...] = jnp.zeros_like(dk)
    dv[...] = jnp.zeros_like(dv)
    first_bytes().wait_recv()
    go(gather(0, 0, 2))

    def stat(h):
        return push(lu.at[h], lu_in.at[h], st_send.at[0, h], st_recv.at[0, h], sib)

    def stat_out(h, k):
        return push(lu_chip.at[h], lu_all.at[h, chip], st_send.at[1, h], st_recv.at[1, h], peer(k))

    def stat_bytes(h):
        block = lu_all.at[h, pl.ds(0, 7)]
        return push(block, block, st_send.at[1, h], st_recv.at[1, h], sib)

    def stat_spread(h):
        stat(h).wait_recv()
        both = lu[h] + lu_in[h]
        lu_chip[h] = both
        lu_all[h, chip] = both
        for k in range(1, 8):
            stat_out(h, k).start()

    def reduce_sib(h):
        src = dq_part.at[h, span_of_rows((1 - core) * half, half, half)]
        return push(src, dq_in0.at[h], rs_send.at[0, h], rs_recv.at[0, h], sib)

    def reduce(h, par, stage):
        if par == 0 and stage == 1:
            src = dq_s0.at[h, span_of_rows((1 - x) * 4 * rows, 4 * rows, 4 * rows)]
            return [push(src, dq_in1.at[h, pl.ds(0, 4 * rows)], rs_send.at[1, h], rs_recv.at[1, h], x_near)]
        if par == 1 and stage == 2:
            src = dq_s1.at[h, span_of_rows((1 - x) * rows, rows, rows)]
            return [push(src, dq_in2.at[h, pl.ds(0, rows)], rs_send.at[2, h], rs_recv.at[2, h], x_near)]
        copies = []
        for k in (1, 2, 3):
            to = around(k)
            if par == 0:
                src = dq_s1.at[h, span_of_rows(to * rows, rows, rows)]
                dst = dq_in2.at[h, pl.ds((3 - k) * rows, rows)]
            else:
                src = dq_s0.at[h, span_of_rows(to * 2 * rows, 2 * rows, 2 * rows)]
                dst = dq_in1.at[h, pl.ds((3 - k) * 2 * rows, 2 * rows)]
            copies.append(push(src, dst, rs_send.at[stage, h], rs_recv.at[stage, h], frame_of(x, to, core)))
        return copies

    def reduce_bytes(h, par, stage):
        count = ((4, 3), (6, 1))[par][stage - 1] * rows
        block = (dq_in1 if stage == 1 else dq_in2).at[h, pl.ds(0, count)]
        return push(block, block, rs_send.at[stage, h], rs_recv.at[stage, h], sib)

    def reduce_first(h, par):
        reduce_sib(h).wait_recv()
        own = dq_part[h, span_of_rows(core * half, half, half)]
        dq_s0[h] = (own.astype(F32) + dq_in0[h].astype(F32)).astype(BF16)
        go(reduce(h, par, 1))

    def reduce_second(h, par):
        reduce_bytes(h, par, 1).wait_recv()
        if par == 0:
            own = dq_s0[h, span_of_rows(x * 4 * rows, 4 * rows, 4 * rows)].astype(F32)
            dq_s1[h] = (own + dq_in1[h, : 4 * rows].astype(F32)).astype(BF16)
        else:
            total = dq_s0[h, span_of_rows(z * 2 * rows, 2 * rows, 2 * rows)].astype(F32)
            for k in range(3):
                total = total + dq_in1[h, k * 2 * rows : (k + 1) * 2 * rows].astype(F32)
            dq_s1[h, : 2 * rows] = total.astype(BF16)
        go(reduce(h, par, 2))

    def finish(h):
        par = h % 2
        reduce_bytes(h, par, 2).wait_recv()
        mine = z if par == 0 else x
        total = dq_s1[h, span_of_rows(mine * rows, rows, rows)].astype(F32)
        for k in range(3 if par == 0 else 1):
            total = total + dq_in2[h, k * rows : (k + 1) * rows].astype(F32)
        at = slice(h * HD, (h + 1) * HD)
        q = q_ref[:, at].astype(F32)
        scale = lax.rsqrt(jnp.mean(q * q, axis=-1, keepdims=True) + EPS)
        g = total * HD ** (-0.5) * qg_ref[...]
        g = scale * g - q * scale**3 * jnp.mean(q * g, axis=-1, keepdims=True)
        dq[:, at] = g.astype(BF16)

    def first_pass(h, par):
        slot = lax.rem(h, SLOTS)
        q, d = qd[h, :, :HD], qd[h, :, HD:]
        l = jnp.zeros((1, every), F32)
        u = jnp.zeros((1, every), F32)
        for m in range(0, keys, CHUNK):
            s = lax.dot_general(kb[m : m + CHUNK], q, NT, preferred_element_type=F32)
            dp = lax.dot_general(v_ref[m : m + CHUNK], d, NT, preferred_element_type=F32)
            live = jnp.concatenate([km[m : m + CHUNK]] * groups, axis=1)
            e = jnp.exp(s) * live
            f = e * dp
            e_buf[slot, m : m + CHUNK] = e.astype(BF16)
            f_buf[slot, m : m + CHUNK] = f.astype(BF16)
            l += jnp.sum(e, axis=0, keepdims=True)
            u += jnp.sum(f, axis=0, keepdims=True)
        l *= rm[par]
        u *= rm[par]
        for j in range(groups):
            lu[h, j : j + 1] = l[:, j * HD : (j + 1) * HD]
            lu[h, groups + j : groups + j + 1] = u[:, j * HD : (j + 1) * HD]

    def row_factors(h, par):
        total = lu_all[h, 0]
        for c in range(1, 8):
            total = total + lu_all[h, c]
        l = jnp.concatenate([total[j : j + 1] for j in range(groups)], axis=1)
        u = jnp.concatenate([total[groups + j : groups + j + 1] for j in range(groups)], axis=1)
        il = rm[par] / l
        return il, (u / l) * il

    def query_grads(h, par):
        slot = lax.rem(h, SLOTS)
        il, w = row_factors(h, par)
        for m in range(0, keys, CHUNK):
            e = e_buf[slot, m : m + CHUNK].astype(F32)
            f = f_buf[slot, m : m + CHUNK].astype(F32)
            f_buf[slot, m : m + CHUNK] = (f * il - e * w).astype(BF16)
        dq_part[h] = jnp.dot(kt[...], f_buf[slot], preferred_element_type=F32).T.astype(BF16)

    def frame_grads(h, par):
        slot = lax.rem(h, SLOTS)
        il, _ = row_factors(h, par)
        col = jnp.concatenate([il] * 8, axis=0).T[:, 0:1]
        d = (qd[h, :, HD:].astype(F32) * col).astype(BF16)
        q = qd[h, :, :HD]
        for m in range(0, keys, CHUNK):
            dv[m : m + CHUNK] += jnp.dot(e_buf[slot, m : m + CHUNK], d, preferred_element_type=F32)
            dk[m : m + CHUNK] += jnp.dot(f_buf[slot, m : m + CHUNK], q, preferred_element_type=F32)

    def step(s, par):
        odd = 1 - par

        @pl.when(s < heads)
        def _():
            gather_bytes(s, par, 2).wait_recv()
            first_pass(s, par)
            stat(s).start()

        @pl.when(s + 1 < heads)
        def _():
            advance(s + 1, odd, 1)

        @pl.when(s + 2 < heads)
        def _():
            advance(s + 2, par, 0)

        @pl.when(s + 3 < heads)
        def _():
            go(gather(s + 3, odd, 0))

        @pl.when(s >= LAG)
        def _():
            stat_bytes(s - LAG).wait_recv()
            query_grads(s - LAG, par)
            reduce_sib(s - LAG).start()

        @pl.when(s < heads)
        def _():
            stat_spread(s)

        @pl.when(s >= LAG)
        def _():
            frame_grads(s - LAG, par)
            reduce_first(s - LAG, par)

        @pl.when(s > LAG)
        def _():
            reduce_second(s - LAG - 1, odd)

    def pair(t, carry):
        step(2 * t, 0)
        step(2 * t + 1, 1)
        return carry

    lax.fori_loop(0, (heads + LAG) // 2, pair, 0)

    for h in range(heads - 2):
        finish(h)
    for t in range(heads):
        pltpu.make_async_copy(w_ref.at[pl.ds(t * cols, cols)], w_buf.at[t], w_sem.at[t]).wait()
    dv_out = pltpu.make_async_copy(dv, dv_ref, out_sem.at[0])
    dv_out.start()
    reduce_second(heads - 1, (heads - 1) % 2)
    k = k_ref[...].astype(F32)
    k_scale = lax.rsqrt(jnp.mean(k * k, axis=-1, keepdims=True) + EPS)
    g = dk[...] * kg_ref[...]
    dk[...] = k_scale * g - k * k_scale**3 * jnp.mean(k * g, axis=-1, keepdims=True)
    dk_out = pltpu.make_async_copy(dk, dk_ref, out_sem.at[1])
    dk_out.start()
    finish(heads - 2)
    finish(heads - 1)

    def text(k):
        return push(t_out.at[k], t_in.at[7 - k], tx_send.at[k], tx_recv.at[7 - k], {"head": group(k)})

    def term(to):
        return lax.dot_general(dq[...], w_buf[to], NT, preferred_element_type=F32)

    for k in (3, 5, 4, 1, 7, 2, 6):
        t_out[k] = term(group(k)).astype(BF16)
        text(k).start()
    total = term(head)

    def drain(h, carry):
        stat(h).wait_send()
        stat_bytes(h).wait_send()
        reduce_sib(h).wait_send()
        gather_bytes(h, 0, 2).wait_send()
        return carry

    def drain_pair(t, carry):
        for par in range(2):
            h = 2 * t + par
            reduce_bytes(h, par, 1).wait_send()
            reduce_bytes(h, par, 2).wait_send()

            @pl.when(h > 0)
            def _():
                gather_bytes(h, par, 0).wait_send()
                gather_bytes(h, par, 1).wait_send()

        return carry

    lax.fori_loop(0, heads, drain, 0)
    lax.fori_loop(0, heads // 2, drain_pair, 0)
    first_bytes().wait_send()
    for k in (4, 2, 3, 6, 0, 5, 1):
        text(7 - k).wait_recv()
        total = total + t_in[k].astype(F32)
    text_ref[...] = total
    for k in range(1, 8):
        text(k).wait_send()
    dv_out.wait()
    dk_out.wait()


def copy_kernel(*refs):
    for src, dst in zip(refs[:3], refs[3:]):
        dst[...] = src[...]


def local(queries, q_gain, keys, k_gain, values, out_grad, w_query, span_mask, frame_len):
    rows, width = queries.shape
    heads = width // HD
    every = lax.axis_size("frame") * rows
    half = every // 2
    n = keys.shape[0]
    cols = w_query.shape[0] // lax.axis_size("head")
    vmem = pl.BlockSpec(memory_space=pltpu.VMEM)
    smem = pl.BlockSpec(memory_space=pltpu.SMEM)
    anywhere = pl.BlockSpec(memory_space=pl.ANY)
    stat = 2 * every // HD
    sems = pltpu.SemaphoreType.DMA
    results = pl.pallas_call(
        functools.partial(kernel, heads, rows),
        out_shape=(
            jax.ShapeDtypeStruct((rows, cols), F32),
            jax.ShapeDtypeStruct((n, HD), F32),
            jax.ShapeDtypeStruct((n, HD), F32),
        ),
        in_specs=[vmem] * 7 + [smem, anywhere],
        out_specs=(vmem, anywhere, anywhere),
        scratch_shapes=[
            pltpu.VMEM((heads, every, 2 * HD), BF16),
            pltpu.VMEM((SLOTS, n, every), BF16),
            pltpu.VMEM((SLOTS, n, every), BF16),
            pltpu.VMEM((n, HD), BF16),
            pltpu.VMEM((HD, n), BF16),
            pltpu.VMEM((n, HD), F32),
            pltpu.VMEM((2, 1, every), F32),
            pltpu.VMEM((n, HD), F32),
            pltpu.VMEM((n, HD), F32),
            pltpu.VMEM((heads, stat, HD), F32),
            pltpu.VMEM((heads, stat, HD), F32),
            pltpu.VMEM((heads, stat, HD), F32),
            pltpu.VMEM((heads, 8, stat, HD), F32),
            pltpu.VMEM((heads, every, HD), BF16),
            pltpu.VMEM((heads, half, HD), BF16),
            pltpu.VMEM((heads, half, HD), BF16),
            pltpu.VMEM((heads, 6 * rows, HD), BF16),
            pltpu.VMEM((heads, 4 * rows, HD), BF16),
            pltpu.VMEM((heads, 3 * rows, HD), BF16),
            pltpu.VMEM((rows, width), BF16),
            pltpu.VMEM((heads, cols, width), BF16),
            pltpu.VMEM((8, rows, cols), BF16),
            pltpu.VMEM((8, rows, cols), BF16),
        ]
        + [sems((3, heads))] * 2
        + [sems((2, heads))] * 2
        + [sems((3, heads))] * 2
        + [sems((8,))] * 2
        + [sems((heads,)), sems((2,))],
        compiler_params=pltpu.CompilerParams(
            collective_id=0, has_side_effects=True, vmem_limit_bytes=62 * 2**20
        ),
        cost_estimate=pl.CostEstimate(
            flops=10 * heads * every * n * HD, bytes_accessed=2**25, transcendentals=heads * every * n
        ),
    )(
        queries, q_gain[None], keys, k_gain[None], values, out_grad, span_mask.reshape(1, -1), frame_len, w_query
    )
    return pl.pallas_call(
        copy_kernel,
        out_shape=[jax.ShapeDtypeStruct(a.shape, a.dtype) for a in results],
        in_specs=[vmem] * 3,
        out_specs=[vmem] * 3,
    )(*results)


def solution(mesh):
    return jax.shard_map(
        local,
        mesh=mesh,
        in_specs=(
            P("frame", "head"), P(), P("frame", "head"), P(), P("frame", "head"),
            P("frame", "head"), P(None, "head"), P(None, "frame"), P("frame"),
        ),
        out_specs=(P("frame", "head"), P("frame", "head"), P("frame", "head")),
        check_vma=False,
    )
```

time: 118 us -> 101 us (0.86)
  Pallas kernels: 77.5 us -> 100 us
  waiting for transfers between devices: 14.7 us -> 0 us
  matrix products: 11.2 us -> 0 us
  starting transfers between devices: 6.53 us -> 0 us
  local copies, waits for them, and re-layouts: 3.36 us -> 0 us
  other arithmetic: 3.23 us -> 0 us
    pallas_call x1 -> x2, Pallas kernels: 77.5 us -> 100 us  [the longest x1 97.2 us: local(): pl.pallas_call(functools.partial(kernel, heads, rows), out_shape=(jax.Sha...]
    all_to_all x1 -> x0, waiting for transfers between devices: 14.7 us -> none  [summed_on_arrival(): lax.all_to_all(parts, axis, split_axis=0, concat_axis=0, tiled=True)]
    dot_general x1 -> x0, matrix products: 11.2 us -> none  [local(): lax.dot_general(dq_raw, w_query, (((1,), (1,)), ((), ())), preferred_elem...]
    all_to_all x1 -> x0, starting transfers between devices: 6.53 us -> none  [summed_on_arrival(): lax.all_to_all(parts, axis, split_axis=0, concat_axis=0, tiled=True)]
    unnamed x10 -> x0, local copies, waits for them, and re-layouts: 2.27 us -> none
    sub x1 -> x0, other arithmetic: 1.83 us -> none  [local(): k_scale * g]
    reduce_sum x2 -> x0, other arithmetic: 1.39 us -> none  [the longest x1 0.87 us: summed_on_arrival(): return arrived.astype(F32).sum(axis=0)]
  transfers between devices with their start and end apart: 1 -> 0, of which waited for: 1 -> 0; matrix products, arithmetic and copies ran while one was open for 2% -> 0% of each run, Pallas kernels for 0% -> 0%
where the time goes in v2:
time: 101 us
  Pallas kernels  100 us (99%)
  between operations  1.29 us (1%)
    pallas_call x1, Pallas kernels, local(): pl.pallas_call(functools.partial(kernel, heads, rows), out_shape=(jax.Sha...  97.2 us
    pallas_call x1, Pallas kernels, local(): pl.pallas_call(copy_kernel, out_shape=[jax.ShapeDtypeStruct(a.shape, a.dt...  2.77 us

profile of v2, /device:TPU:1, one launch (start us, length us, event | category | flops | bytes accessed | tf_op | source)
XLA Modules:
  0.0 101.3 jit_solution(15164544363885074233)
XLA Ops:
  1.3 97.2 %shard_map.112 = (f32[64,1024]{1,0:T(8,128)}, f32[1600,128]{1,0:T(8,128)}, f32[1600,128]{1,0:T(8,128)}) custom-call(bf16[64,1024]{1,0:T(8,128)(2,1)} %q_ref.1, f32[1,128]{1,0:T(1,128)} %bitcast.3, bf16[1600,128]{1,0:T(8,128)(2,1)} %k_ref.1, f32[1,128]{1,0:T(1,128)} %bitcast.4, bf16[1600,128]{1,0:T(8,128)(2,1)} %v_ref.1, bf16[64,1024]{1,0:T(8,128)(2,1)} %d_ref.1, ...), custom_call_target="tpu_custom_call" | custom-call | flops 16777216000 | bytes 33554432 | tf_op jit(solution)/shard_map/pallas_call | solution.py:401
  98.5 2.8 %shard_map.113 = (f32[64,1024]{1,0:T(8,128)}, f32[1600,128]{1,0:T(8,128)}, f32[1600,128]{1,0:T(8,128)}) custom-call(f32[64,1024]{1,0:T(8,128)} %get-tuple-element.6.refs_0_, f32[1600,128]{1,0:T(8,128)} %get-tuple-element.7.refs_1_, f32[1600,128]{1,0:T(8,128)} %get-tuple-element.8.refs_2_), custom_call_target="tpu_custom_call" | custom-call | tf_op jit(solution)/shard_map/pallas_call | solution.py:449

commit v3 on v2

--- a/solution.py
+++ b/solution.py
@@ -14,6 +14,7 @@
 LAG = 2
 SLOTS = LAG + 1
 CHUNK = 320
+DIRECT = 4
 F32 = jnp.float32
 BF16 = jnp.bfloat16
 NT = (((1,), (1,)), ((), ()))
@@ -23,7 +24,7 @@
     heads, rows, q_ref, qg_ref, k_ref, kg_ref, v_ref, d_ref, span_ref, len_ref, w_ref,
     text_ref, dk_ref, dv_ref,
     qd, e_buf, f_buf, kb, kt, km, rm, dk, dv, lu, lu_in, lu_chip, lu_all, dq_part, dq_in0, dq_s0, dq_in1, dq_s1,
-    dq_in2, dq, w_buf, t_out, t_in,
+    dq_in2, dq_last, dq, w_buf, t_sum, t_out, t_in,
     ag_send, ag_recv, st_send, st_recv, rs_send, rs_recv, tx_send, tx_recv, w_sem, out_sem,
 ):
     frame = lax.axis_index("frame")
@@ -106,22 +107,22 @@
         qd[h, mine, :HD] = (q * scale * qg_ref[...] * HD ** (-0.5)).astype(BF16)
         qd[h, mine, HD:] = d_ref[:, at]
 
-    def first_block(k):
-        block = qd.at[0, span_of_rows(core * half + index(0, x, z) * rows, rows, rows)]
-        return push(block, block, ag_send.at[0, 0], ag_recv.at[0, 0], peer(k))
-
-    def first_bytes():
-        block = qd.at[0, pl.ds(0, 7 * rows)]
-        return push(block, block, ag_send.at[0, 0], ag_recv.at[0, 0], sib)
+    def direct(h, par, k):
+        block = qd.at[h, span_of_rows(core * half + index(par, x, z) * rows, rows, rows)]
+        return push(block, block, ag_send.at[0, h], ag_recv.at[0, h], peer(k))
+
+    def direct_bytes(h):
+        block = qd.at[h, pl.ds(0, 7 * rows)]
+        return push(block, block, ag_send.at[0, h], ag_recv.at[0, h], sib)
 
     head_rows(0)
     pl.semaphore_wait(barrier, 15)
-    for k in range(1, 8):
-        first_block(k).start()
-    head_rows(1)
-    go(gather(1, 1, 0))
-    for h in range(2, heads):
-        head_rows(h)
+    for h in range(heads):
+        if h > 0:
+            head_rows(h)
+        if h < DIRECT:
+            for k in range(1, 8):
+                direct(h, h % 2, k).start()
     for t in range(heads):
         pltpu.make_async_copy(w_ref.at[pl.ds(t * cols, cols)], w_buf.at[t], w_sem.at[t]).start()
 
@@ -130,8 +131,6 @@
     k = k * k_scale * kg_ref[...]
     kb[...] = k.astype(BF16)
     kt[...] = k.T.astype(BF16)
-    advance(1, 1, 0)
-    go(gather(2, 0, 0))
     km[...] = (lax.broadcasted_iota(jnp.int32, km.shape, 0) < len_ref[0]).astype(F32)
     spans = span_ref.shape[1]
     r = lax.broadcasted_iota(jnp.int32, (spans, every), 1)
@@ -144,7 +143,7 @@
         rm[par] = jnp.dot(seen, hit, preferred_element_type=F32)[0:1]
     dk[...] = jnp.zeros_like(dk)
     dv[...] = jnp.zeros_like(dv)
-    first_bytes().wait_recv()
+    direct_bytes(0).wait_recv()
     go(gather(0, 0, 2))
 
     def stat(h):
@@ -193,11 +192,30 @@
         block = (dq_in1 if stage == 1 else dq_in2).at[h, pl.ds(0, count)]
         return push(block, block, rs_send.at[stage, h], rs_recv.at[stage, h], sib)
 
+    def last(k):
+        to = lax.rem(chip + k, 8)
+        src = dq_s0.at[heads - 1, span_of_rows(index(1, to // 4, lax.rem(to, 4)) * rows, rows, rows)]
+        return push(src, dq_last.at[7 - k], rs_send.at[1, heads - 1], rs_recv.at[1, heads - 1], peer(k))
+
+    def last_bytes():
+        block = dq_last.at[pl.ds(0, 7)]
+        return push(block, block, rs_send.at[1, heads - 1], rs_recv.at[1, heads - 1], sib)
+
     def reduce_first(h, par):
         reduce_sib(h).wait_recv()
         own = dq_part[h, span_of_rows(core * half, half, half)]
         dq_s0[h] = (own.astype(F32) + dq_in0[h].astype(F32)).astype(BF16)
-        go(reduce(h, par, 1))
+
+        @pl.when(h < heads - 1)
+        def _():
+            go(reduce(h, par, 1))
+
+        if par == 1:
+
+            @pl.when(h == heads - 1)
+            def _():
+                for k in range(1, 8):
+                    last(k).start()
 
     def reduce_second(h, par):
         reduce_bytes(h, par, 1).wait_recv()
@@ -213,11 +231,17 @@
 
     def finish(h):
         par = h % 2
-        reduce_bytes(h, par, 2).wait_recv()
-        mine = z if par == 0 else x
-        total = dq_s1[h, span_of_rows(mine * rows, rows, rows)].astype(F32)
-        for k in range(3 if par == 0 else 1):
-            total = total + dq_in2[h, k * rows : (k + 1) * rows].astype(F32)
+        if h == heads - 1:
+            last_bytes().wait_recv()
+            total = dq_s0[h, span_of_rows(index(1, x, z) * rows, rows, rows)].astype(F32)
+            for k in range(7):
+                total = total + dq_last[k].astype(F32)
+        else:
+            reduce_bytes(h, par, 2).wait_recv()
+            mine = z if par == 0 else x
+            total = dq_s1[h, span_of_rows(mine * rows, rows, rows)].astype(F32)
+            for k in range(3 if par == 0 else 1):
+                total = total + dq_in2[h, k * rows : (k + 1) * rows].astype(F32)
         at = slice(h * HD, (h + 1) * HD)
         q = q_ref[:, at].astype(F32)
         scale = lax.rsqrt(jnp.mean(q * q, axis=-1, keepdims=True) + EPS)
@@ -225,7 +249,7 @@
         g = scale * g - q * scale**3 * jnp.mean(q * g, axis=-1, keepdims=True)
         dq[:, at] = g.astype(BF16)
 
-    def first_pass(h, par):
+    def first_pass(h, par, between):
         slot = lax.rem(h, SLOTS)
         q, d = qd[h, :, :HD], qd[h, :, HD:]
         l = jnp.zeros((1, every), F32)
@@ -240,6 +264,8 @@
             f_buf[slot, m : m + CHUNK] = f.astype(BF16)
             l += jnp.sum(e, axis=0, keepdims=True)
             u += jnp.sum(f, axis=0, keepdims=True)
+            if m == 2 * CHUNK:
+                between()
         l *= rm[par]
         u *= rm[par]
         for j in range(groups):
@@ -255,50 +281,55 @@
         il = rm[par] / l
         return il, (u / l) * il
 
-    def query_grads(h, par):
+    def score_grads(h, par):
         slot = lax.rem(h, SLOTS)
         il, w = row_factors(h, par)
-        for m in range(0, keys, CHUNK):
-            e = e_buf[slot, m : m + CHUNK].astype(F32)
-            f = f_buf[slot, m : m + CHUNK].astype(F32)
-            f_buf[slot, m : m + CHUNK] = (f * il - e * w).astype(BF16)
-        dq_part[h] = jnp.dot(kt[...], f_buf[slot], preferred_element_type=F32).T.astype(BF16)
-
-    def frame_grads(h, par):
-        slot = lax.rem(h, SLOTS)
-        il, _ = row_factors(h, par)
         col = jnp.concatenate([il] * 8, axis=0).T[:, 0:1]
         d = (qd[h, :, HD:].astype(F32) * col).astype(BF16)
+        for m in range(0, keys, CHUNK):
+            e = e_buf[slot, m : m + CHUNK]
+            f = f_buf[slot, m : m + CHUNK].astype(F32)
+            f_buf[slot, m : m + CHUNK] = (f * il - e.astype(F32) * w).astype(BF16)
+            dv[m : m + CHUNK] += jnp.dot(e, d, preferred_element_type=F32)
+        dq_part[h] = jnp.dot(kt[...], f_buf[slot], preferred_element_type=F32).T.astype(BF16)
+
+    def key_grads(h):
+        slot = lax.rem(h, SLOTS)
         q = qd[h, :, :HD]
         for m in range(0, keys, CHUNK):
-            dv[m : m + CHUNK] += jnp.dot(e_buf[slot, m : m + CHUNK], d, preferred_element_type=F32)
             dk[m : m + CHUNK] += jnp.dot(f_buf[slot, m : m + CHUNK], q, preferred_element_type=F32)
 
     def step(s, par):
         odd = 1 - par
 
+        def forward():
+            @pl.when(s + 1 < DIRECT)
+            def _():
+                direct_bytes(s + 1).wait_recv()
+                go(gather(s + 1, odd, 2))
+
+            @pl.when((s + 1 >= DIRECT) & (s + 1 < heads))
+            def _():
+                advance(s + 1, odd, 1)
+
         @pl.when(s < heads)
         def _():
             gather_bytes(s, par, 2).wait_recv()
-            first_pass(s, par)
+            first_pass(s, par, forward)
             stat(s).start()
 
-        @pl.when(s + 1 < heads)
-        def _():
-            advance(s + 1, odd, 1)
-
-        @pl.when(s + 2 < heads)
+        @pl.when((s + 2 >= DIRECT) & (s + 2 < heads))
         def _():
             advance(s + 2, par, 0)
 
-        @pl.when(s + 3 < heads)
+        @pl.when((s + 3 >= DIRECT) & (s + 3 < heads))
         def _():
             go(gather(s + 3, odd, 0))
 
         @pl.when(s >= LAG)
         def _():
             stat_bytes(s - LAG).wait_recv()
-            query_grads(s - LAG, par)
+            score_grads(s - LAG, par)
             reduce_sib(s - LAG).start()
 
         @pl.when(s < heads)
@@ -307,7 +338,7 @@
 
         @pl.when(s >= LAG)
         def _():
-            frame_grads(s - LAG, par)
+            key_grads(s - LAG)
             reduce_first(s - LAG, par)
 
         @pl.when(s > LAG)
@@ -327,7 +358,13 @@
         pltpu.make_async_copy(w_ref.at[pl.ds(t * cols, cols)], w_buf.at[t], w_sem.at[t]).wait()
     dv_out = pltpu.make_async_copy(dv, dv_ref, out_sem.at[0])
     dv_out.start()
-    reduce_second(heads - 1, (heads - 1) % 2)
+    ready = (heads - 2) * HD
+
+    def early(t):
+        t_sum[t] = lax.dot_general(dq[:, :ready], w_buf[t, :, :ready], NT, preferred_element_type=F32)
+
+    for t in range(8):
+        early(t)
     k = k_ref[...].astype(F32)
     k_scale = lax.rsqrt(jnp.mean(k * k, axis=-1, keepdims=True) + EPS)
     g = dk[...] * kg_ref[...]
@@ -341,7 +378,8 @@
         return push(t_out.at[k], t_in.at[7 - k], tx_send.at[k], tx_recv.at[7 - k], {"head": group(k)})
 
     def term(to):
-        return lax.dot_general(dq[...], w_buf[to], NT, preferred_element_type=F32)
+        late = lax.dot_general(dq[:, ready:], w_buf[to, :, ready:], NT, preferred_element_type=F32)
+        return t_sum[to] + late
 
     for k in (3, 5, 4, 1, 7, 2, 6):
         t_out[k] = term(group(k)).astype(BF16)
@@ -358,10 +396,17 @@
     def drain_pair(t, carry):
         for par in range(2):
             h = 2 * t + par
-            reduce_bytes(h, par, 1).wait_send()
-            reduce_bytes(h, par, 2).wait_send()
-
-            @pl.when(h > 0)
+
+            @pl.when(h < heads - 1)
+            def _():
+                reduce_bytes(h, par, 1).wait_send()
+                reduce_bytes(h, par, 2).wait_send()
+
+            @pl.when(h < DIRECT)
+            def _():
+                direct_bytes(h).wait_send()
+
+            @pl.when(h >= DIRECT)
             def _():
                 gather_bytes(h, par, 0).wait_send()
                 gather_bytes(h, par, 1).wait_send()
@@ -370,7 +415,7 @@
 
     lax.fori_loop(0, heads, drain, 0)
     lax.fori_loop(0, heads // 2, drain_pair, 0)
-    first_bytes().wait_send()
+    last_bytes().wait_send()
     for k in (4, 2, 3, 6, 0, 5, 1):
         text(7 - k).wait_recv()
         total = total + t_in[k].astype(F32)
@@ -427,8 +472,10 @@
             pltpu.VMEM((heads, 6 * rows, HD), BF16),
             pltpu.VMEM((heads, 4 * rows, HD), BF16),
             pltpu.VMEM((heads, 3 * rows, HD), BF16),
+            pltpu.VMEM((7, rows, HD), BF16),
             pltpu.VMEM((rows, width), BF16),
             pltpu.VMEM((heads, cols, width), BF16),
+            pltpu.VMEM((8, rows, cols), F32),
             pltpu.VMEM((8, rows, cols), BF16),
             pltpu.VMEM((8, rows, cols), BF16),
         ]

time: 101 us -> 97.9 us (0.969)
  Pallas kernels: 100 us -> 96.4 us
    pallas_call x1, Pallas kernels: 97.2 us -> 93.6 us  [local(): pl.pallas_call(functools.partial(kernel, heads, rows), out_shape=(jax.Sha...]
where the time goes in v3:
time: 97.9 us; the launch traced here: 97.7 us
  Pallas kernels  96.4 us (98%)
  between operations  1.29 us (1%)
    pallas_call x1, Pallas kernels, local(): pl.pallas_call(functools.partial(kernel, heads, rows), out_shape=(jax.Sha...  93.6 us
    pallas_call x1, Pallas kernels, local(): pl.pallas_call(copy_kernel, out_shape=[jax.ShapeDtypeStruct(a.shape, a.dt...  2.77 us

profile of v3, /device:TPU:1, one launch (start us, length us, event | category | flops | bytes accessed | tf_op | source)
XLA Modules:
  0.0 97.7 jit_solution(5406001467096487040)
XLA Ops:
  1.3 93.6 %shard_map.112 = (f32[64,1024]{1,0:T(8,128)}, f32[1600,128]{1,0:T(8,128)}, f32[1600,128]{1,0:T(8,128)}) custom-call(bf16[64,1024]{1,0:T(8,128)(2,1)} %q_ref.1, f32[1,128]{1,0:T(1,128)} %bitcast.3, bf16[1600,128]{1,0:T(8,128)(2,1)} %k_ref.1, f32[1,128]{1,0:T(1,128)} %bitcast.4, bf16[1600,128]{1,0:T(8,128)(2,1)} %v_ref.1, bf16[64,1024]{1,0:T(8,128)(2,1)} %d_ref.1, ...), custom_call_target="tpu_custom_call" | custom-call | flops 16777216000 | bytes 33554432 | tf_op jit(solution)/shard_map/pallas_call | solution.py:446
  94.9 2.8 %shard_map.113 = (f32[64,1024]{1,0:T(8,128)}, f32[1600,128]{1,0:T(8,128)}, f32[1600,128]{1,0:T(8,128)}) custom-call(f32[64,1024]{1,0:T(8,128)} %get-tuple-element.6.refs_0_, f32[1600,128]{1,0:T(8,128)} %get-tuple-element.7.refs_1_, f32[1600,128]{1,0:T(8,128)} %get-tuple-element.8.refs_2_), custom_call_target="tpu_custom_call" | custom-call | tf_op jit(solution)/shard_map/pallas_call | solution.py:496

commit v4 on v3

--- a/solution.py
+++ b/solution.py
@@ -192,30 +192,30 @@
         block = (dq_in1 if stage == 1 else dq_in2).at[h, pl.ds(0, count)]
         return push(block, block, rs_send.at[stage, h], rs_recv.at[stage, h], sib)
 
-    def last(k):
+    def last(par, k):
+        h = heads - 2 + par
         to = lax.rem(chip + k, 8)
-        src = dq_s0.at[heads - 1, span_of_rows(index(1, to // 4, lax.rem(to, 4)) * rows, rows, rows)]
-        return push(src, dq_last.at[7 - k], rs_send.at[1, heads - 1], rs_recv.at[1, heads - 1], peer(k))
-
-    def last_bytes():
-        block = dq_last.at[pl.ds(0, 7)]
-        return push(block, block, rs_send.at[1, heads - 1], rs_recv.at[1, heads - 1], sib)
+        src = dq_s0.at[h, span_of_rows(index(par, to // 4, lax.rem(to, 4)) * rows, rows, rows)]
+        return push(src, dq_last.at[par, 7 - k], rs_send.at[1, h], rs_recv.at[1, h], peer(k))
+
+    def last_bytes(par):
+        block = dq_last.at[par, pl.ds(0, 7)]
+        h = heads - 2 + par
+        return push(block, block, rs_send.at[1, h], rs_recv.at[1, h], sib)
 
     def reduce_first(h, par):
         reduce_sib(h).wait_recv()
         own = dq_part[h, span_of_rows(core * half, half, half)]
         dq_s0[h] = (own.astype(F32) + dq_in0[h].astype(F32)).astype(BF16)
 
-        @pl.when(h < heads - 1)
+        @pl.when(h < heads - 2)
         def _():
             go(reduce(h, par, 1))
 
-        if par == 1:
-
-            @pl.when(h == heads - 1)
-            def _():
-                for k in range(1, 8):
-                    last(k).start()
+        @pl.when(h >= heads - 2)
+        def _():
+            for k in range(1, 8):
+                last(par, k).start()
 
     def reduce_second(h, par):
         reduce_bytes(h, par, 1).wait_recv()
@@ -231,11 +231,11 @@
 
     def finish(h):
         par = h % 2
-        if h == heads - 1:
-            last_bytes().wait_recv()
-            total = dq_s0[h, span_of_rows(index(1, x, z) * rows, rows, rows)].astype(F32)
+        if h >= heads - 2:
+            last_bytes(par).wait_recv()
+            total = dq_s0[h, span_of_rows(index(par, x, z) * rows, rows, rows)].astype(F32)
             for k in range(7):
-                total = total + dq_last[k].astype(F32)
+                total = total + dq_last[par, k].astype(F32)
         else:
             reduce_bytes(h, par, 2).wait_recv()
             mine = z if par == 0 else x
@@ -281,7 +281,7 @@
         il = rm[par] / l
         return il, (u / l) * il
 
-    def score_grads(h, par):
+    def second_pass(h, par):
         slot = lax.rem(h, SLOTS)
         il, w = row_factors(h, par)
         col = jnp.concatenate([il] * 8, axis=0).T[:, 0:1]
@@ -291,13 +291,11 @@
             f = f_buf[slot, m : m + CHUNK].astype(F32)
             f_buf[slot, m : m + CHUNK] = (f * il - e.astype(F32) * w).astype(BF16)
             dv[m : m + CHUNK] += jnp.dot(e, d, preferred_element_type=F32)
-        dq_part[h] = jnp.dot(kt[...], f_buf[slot], preferred_element_type=F32).T.astype(BF16)
-
-    def key_grads(h):
-        slot = lax.rem(h, SLOTS)
+        dqt = jnp.dot(kt[...], f_buf[slot], preferred_element_type=F32)
         q = qd[h, :, :HD]
         for m in range(0, keys, CHUNK):
             dk[m : m + CHUNK] += jnp.dot(f_buf[slot, m : m + CHUNK], q, preferred_element_type=F32)
+        dq_part[h] = dqt.T.astype(BF16)
 
     def step(s, par):
         odd = 1 - par
@@ -326,24 +324,23 @@
         def _():
             go(gather(s + 3, odd, 0))
 
+        @pl.when(s > LAG)
+        def _():
+            reduce_first(s - LAG - 1, odd)
+
+        @pl.when(s > LAG + 1)
+        def _():
+            reduce_second(s - LAG - 2, par)
+
         @pl.when(s >= LAG)
         def _():
             stat_bytes(s - LAG).wait_recv()
-            score_grads(s - LAG, par)
+            second_pass(s - LAG, par)
             reduce_sib(s - LAG).start()
 
         @pl.when(s < heads)
         def _():
             stat_spread(s)
-
-        @pl.when(s >= LAG)
-        def _():
-            key_grads(s - LAG)
-            reduce_first(s - LAG, par)
-
-        @pl.when(s > LAG)
-        def _():
-            reduce_second(s - LAG - 1, odd)
 
     def pair(t, carry):
         step(2 * t, 0)
@@ -363,7 +360,9 @@
     def early(t):
         t_sum[t] = lax.dot_general(dq[:, :ready], w_buf[t, :, :ready], NT, preferred_element_type=F32)
 
-    for t in range(8):
+    early(0)
+    reduce_first(heads - 1, 1)
+    for t in range(1, 8):
         early(t)
     k = k_ref[...].astype(F32)
     k_scale = lax.rsqrt(jnp.mean(k * k, axis=-1, keepdims=True) + EPS)
@@ -397,7 +396,7 @@
         for par in range(2):
             h = 2 * t + par
 
-            @pl.when(h < heads - 1)
+            @pl.when(h < heads - 2)
             def _():
                 reduce_bytes(h, par, 1).wait_send()
                 reduce_bytes(h, par, 2).wait_send()
@@ -415,7 +414,8 @@
 
     lax.fori_loop(0, heads, drain, 0)
     lax.fori_loop(0, heads // 2, drain_pair, 0)
-    last_bytes().wait_send()
+    last_bytes(0).wait_send()
+    last_bytes(1).wait_send()
     for k in (4, 2, 3, 6, 0, 5, 1):
         text(7 - k).wait_recv()
         total = total + t_in[k].astype(F32)
@@ -472,7 +472,7 @@
             pltpu.VMEM((heads, 6 * rows, HD), BF16),
             pltpu.VMEM((heads, 4 * rows, HD), BF16),
             pltpu.VMEM((heads, 3 * rows, HD), BF16),
-            pltpu.VMEM((7, rows, HD), BF16),
+            pltpu.VMEM((2, 7, rows, HD), BF16),
             pltpu.VMEM((rows, width), BF16),
             pltpu.VMEM((heads, cols, width), BF16),
             pltpu.VMEM((8, rows, cols), F32),

time: 97.9 us -> 94.4 us (0.964)
  Pallas kernels: 96.4 us -> 92.7 us
    pallas_call x1, Pallas kernels: 93.6 us -> 89.9 us  [local(): pl.pallas_call(functools.partial(kernel, heads, rows), out_shape=(jax.Sha...]
where the time goes in v4:
time: 94.4 us; the launch traced here: 94 us
  Pallas kernels  92.7 us (98%)
  between operations  1.29 us (1%)
    pallas_call x1, Pallas kernels, local(): pl.pallas_call(functools.partial(kernel, heads, rows), out_shape=(jax.Sha...  89.9 us
    pallas_call x1, Pallas kernels, local(): pl.pallas_call(copy_kernel, out_shape=[jax.ShapeDtypeStruct(a.shape, a.dt...  2.77 us

profile of v4, /device:TPU:1, one launch (start us, length us, event | category | flops | bytes accessed | tf_op | source)
XLA Modules:
  0.0 94.0 jit_solution(11687316955759131569)
XLA Ops:
  1.3 89.9 %shard_map.112 = (f32[64,1024]{1,0:T(8,128)}, f32[1600,128]{1,0:T(8,128)}, f32[1600,128]{1,0:T(8,128)}) custom-call(bf16[64,1024]{1,0:T(8,128)(2,1)} %q_ref.1, f32[1,128]{1,0:T(1,128)} %bitcast.3, bf16[1600,128]{1,0:T(8,128)(2,1)} %k_ref.1, f32[1,128]{1,0:T(1,128)} %bitcast.4, bf16[1600,128]{1,0:T(8,128)(2,1)} %v_ref.1, bf16[64,1024]{1,0:T(8,128)(2,1)} %d_ref.1, ...), custom_call_target="tpu_custom_call" | custom-call | flops 16777216000 | bytes 33554432 | tf_op jit(solution)/shard_map/pallas_call | solution.py:446
  91.2 2.8 %shard_map.113 = (f32[64,1024]{1,0:T(8,128)}, f32[1600,128]{1,0:T(8,128)}, f32[1600,128]{1,0:T(8,128)}) custom-call(f32[64,1024]{1,0:T(8,128)} %get-tuple-element.6.refs_0_, f32[1600,128]{1,0:T(8,128)} %get-tuple-element.7.refs_1_, f32[1600,128]{1,0:T(8,128)} %get-tuple-element.8.refs_2_), custom_call_target="tpu_custom_call" | custom-call | tf_op jit(solution)/shard_map/pallas_call | solution.py:496
